TPU v7x, 256 devices: a whole 4x4x8 slice. The times are simulated.
256 devices in a mesh: row: 16 (over z, core), col: 16 (over x, y).
Axes of the slice: x: 4, y: 4, z: 8, core: 2. Of those that a mesh axis runs over, the one named last changes fastest.
Arguments:
- start: float32 [2048, 1024], P(('row', 'col'))
- stiff: float32 [2048, 64, 576], P(('row', 'col'))
- convect: float32 [2048, 64, 64], P(('row', 'col')), may hold values from -0.1875 to 0.1875
- column_index: int32 [2048, 9], P(('row', 'col')), may hold values from 0 to 2047, as said below
- upwind: int32 [2048, 9], P(('row', 'col')), may hold values 0 or 1
Outputs:
- basis_first: float32 [2048, 5120], P(('row', 'col'))
- basis_second: float32 [2048, 4096], P(('row', 'col'))
- factor_first: float32 [80, 80], replicated
- coupling: float32 [80, 64], replicated
- factor_second: float32 [64, 64], replicated
Inputs may be any that keep to these rules, and one draw needn't show every extreme that they name: `column_index`: slot 0 of block row b is b itself. Slots 1 to 6 lie in the block row's own sector (block rows s * 128 to (s + 1) * 128 - 1 for sector s), slot 7 in the previous sector and slot 8 in the next one, cyclically over the 16 sectors.
All inputs are finite; a program needn't handle non-finite values. No bound on the sum of `upwind` on one device may be relied on, other than what follows from the above.
Results may differ from a plain program's by a relative error of at most 0.0003.
Values sent between devices are 32-bit elements; how exact they have to be, the bound alone decides.
A program may use at most 128 MiB of HBM per device.

v0:
```python
import jax
import jax.numpy as jnp
from jax import lax
from jax.sharding import PartitionSpec as P

STEPS = 4


def from_behind(x, axis, by):
    peers = lax.axis_size(axis)
    return lax.ppermute(x, axis, [(i, (i + by) % peers) for i in range(peers)])


def finish(panel, lower):
    width = lower.shape[0]
    inverse = jax.scipy.linalg.solve_triangular(
        lower, jnp.eye(width, dtype=jnp.float32), lower=True
    )
    basis = jnp.einsum("pq,bqi->bpi", inverse, panel, precision=lax.Precision.HIGHEST)
    return (basis, lower.T)


def factor_panel(panel, total_rows):
    local_gram = jnp.einsum("bpi,bqi->pq", panel, panel, precision=lax.Precision.HIGHEST)
    gram_all = lax.psum(local_gram, ("row", "col")) / total_rows
    lower = jnp.linalg.cholesky(gram_all)
    return finish(panel, lower)


def per_device(start, stiff, convect, column_index, upwind):
    row_count = lax.axis_size("row")
    col_count = lax.axis_size("col")
    sector = lax.axis_index("row")
    block_rows = start.shape[0]
    slot_count = column_index.shape[1]
    block_size = stiff.shape[1]
    rhs_count = start.shape[1] // block_size
    group_size = block_rows * col_count
    total_rows = block_rows * row_count * col_count * block_size
    own_first = sector * group_size
    prev_first = (sector + row_count - 1) % row_count * group_size
    next_first = (sector + 1) % row_count * group_size
    slot_ids = lax.broadcasted_iota(jnp.int32, column_index.shape, 1)
    slot_pos = jnp.where(
        slot_ids == slot_count - 2,
        group_size + column_index - prev_first,
        jnp.where(
            slot_ids == slot_count - 1,
            2 * group_size + column_index - next_first,
            column_index - own_first,
        ),
    )
    weights = stiff.reshape(block_rows, block_size, slot_count, block_size)
    flag_f = upwind.astype(jnp.float32)
    flag_total = jnp.sum(flag_f, axis=1)[:, None, None]

    def apply_matrix(vector):
        own_group = lax.all_gather(vector, "col", axis=0, tiled=True)
        prev_group = from_behind(own_group, "row", 1)
        next_group = from_behind(own_group, "row", -1)
        whole = jnp.concatenate([own_group, prev_group, next_group], 0)
        near = jnp.take(whole, slot_pos, axis=0).reshape(
            block_rows, slot_count, rhs_count, block_size
        )
        field = vector.reshape(block_rows, rhs_count, block_size)
        result = jnp.einsum("bijk,bjrk->bri", weights, near, precision=lax.Precision.HIGHEST)
        upwind_sum = jnp.einsum("bj,bjrk->brk", flag_f, near, precision=lax.Precision.HIGHEST)
        upwind_diff = upwind_sum - flag_total * field
        result = result + jnp.einsum(
            "bik,brk->bri", convect, upwind_diff, precision=lax.Precision.HIGHEST
        )
        return result.reshape(block_rows, rhs_count * block_size)

    def powers(first, include):
        current = first
        pieces = [first] if include else []
        for section in range(STEPS):
            current = apply_matrix(current)
            pieces.append(current)
        stacked = jnp.stack(
            [piece.reshape(block_rows, rhs_count, block_size) for piece in pieces], 1
        )
        return stacked.reshape(block_rows, len(pieces) * rhs_count, block_size)

    panel = powers(start, True)
    basis_one, factor_one = factor_panel(panel, total_rows)
    last_block = basis_one[:, STEPS * rhs_count :, :].reshape(block_rows, rhs_count * block_size)
    fresh = powers(last_block, False)
    local_coupling = jnp.einsum("bpi,bqi->pq", basis_one, fresh, precision=lax.Precision.HIGHEST)
    coupling = lax.psum(local_coupling, ("row", "col")) / total_rows
    projected = fresh - jnp.einsum(
        "pq,bpi->bqi", coupling, basis_one, precision=lax.Precision.HIGHEST
    )
    basis_two, factor_two = factor_panel(projected, total_rows)
    return (
        basis_one.reshape(block_rows, -1),
        basis_two.reshape(block_rows, -1),
        factor_one,
        coupling,
        factor_two,
    )


def solution(mesh):
    return jax.shard_map(
        per_device,
        mesh=mesh,
        in_specs=(
            P(("row", "col"), None),
            P(("row", "col"), None, None),
            P(("row", "col"), None, None),
            P(("row", "col"), None),
            P(("row", "col"), None),
        ),
        out_specs=(P(("row", "col"), None), P(("row", "col"), None), P(), P(), P()),
        check_vma=False,
    )
```

profile of v0, /device:TPU:1, one launch (start us, length us, event | category | flops | bytes accessed | tf_op | source)
XLA Modules:
  0.0 605.8 jit_solution(431270361540008213)
XLA Ops:
  0.6 20.1 %all_gather.24 = f32[128,1024]{1,0:T(8,128)S(1)} all-gather(f32[8,1024]{1,0:T(8,128)} %param.7), channel_id=1, replica_groups=mesh['row'=16,'col'=16] {'col'}, dimensions={0}, use_global_device_ids=true | all-gather | bytes 557056 | tf_op jit(solution)/shard_map/all_gather | solution.py:58
  20.7 7.3 %collective-permute-start = (f32[128,1024]{1,0:T(8,128)S(1)}, f32[128,1024]{1,0:T(8,128)}, u32[]{:S(2)}, u32[]{:S(2)}) collective-permute-start(f32[128,1024]{1,0:T(8,128)S(1)} %all_gather.24), channel_id=1, source_target_pairs={{0,16},{16,32},{32,48},{48,64},{64,80},{80,96},{96,112},{112,128},... | collective-permute-start | bytes 1572872 | tf_op jit(solution)/shard_map/ppermute | solution.py:11
  34.2 2.6 collective-permute-done.1
  36.8 2.5 pad_maximum_fusion
  39.3 2.2 gather_fusion
  46.0 18.3 %all_gather.25 = f32[128,1024]{1,0:T(8,128)S(1)} all-gather(f32[8,1024]{1,0:T(8,128)S(1)} %reshape.101), channel_id=1, replica_groups=mesh['row'=16,'col'=16] {'col'}, dimensions={0}, use_global_device_ids=true | all-gather | bytes 557056 | tf_op jit(solution)/shard_map/all_gather | solution.py:58
  64.3 5.1 collective-permute-start.2
  69.4 6.1 %collective-permute-done.2 = f32[128,1024]{1,0:T(8,128)S(1)} collective-permute-done((f32[128,1024]{1,0:T(8,128)S(1)}, f32[128,1024]{1,0:T(8,128)S(1)}, u32[]{:S(2)}, u32[]{:S(2)}) %collective-permute-start.2) | collective-permute-done | bytes 524320 | tf_op jit(solution)/shard_map/ppermute | solution.py:11
  75.5 2.8 collective-permute-done.3
  79.6 2.2 gather_fusion.1
  86.2 16.9 %all_gather.26 = f32[128,1024]{1,0:T(8,128)S(1)} all-gather(f32[8,1024]{1,0:T(8,128)S(1)} %reshape.103), channel_id=1, replica_groups=mesh['row'=16,'col'=16] {'col'}, dimensions={0}, use_global_device_ids=true | all-gather | bytes 557056 | tf_op jit(solution)/shard_map/all_gather | solution.py:58
  103.2 5.1 collective-permute-start.4
  108.8 5.6 collective-permute-done.4
  114.4 2.8 collective-permute-done.5
  118.4 2.2 gather_fusion.2
  125.1 18.1 %all_gather.27 = f32[128,1024]{1,0:T(8,128)S(1)} all-gather(f32[8,1024]{1,0:T(8,128)S(1)} %reshape.105), channel_id=1, replica_groups=mesh['row'=16,'col'=16] {'col'}, dimensions={0}, use_global_device_ids=true | all-gather | bytes 557056 | tf_op jit(solution)/shard_map/all_gather | solution.py:58
  143.2 4.9 collective-permute-start.6
  150.1 4.1 collective-permute-done.6
  154.2 2.8 collective-permute-done.7
  158.3 2.2 gather_fusion.3
  166.3 81.9 %psum.21 = f32[80,80]{0,1:T(8,128)S(1)} all-reduce(f32[80,80]{0,1:T(8,128)S(1)} %convolution_bitcast_fusion.4), channel_id=1, replica_groups=mesh['row'=16,'col'=16] {'row','col'}, use_global_device_ids=true, to_apply=%region_1.3 | all-reduce | flops 6400 | bytes 51200 | tf_op jit(solution)/shard_map/psum | solution.py:25
  248.3 7.3 %cholesky.31 = f32[80,80]{1,0:T(8,128)S(1)} custom-call(f32[80,80]{1,0:T(8,128)S(1)} %fusion.77), custom_call_target="Cholesky" | custom-call | tf_op jit(solution)/shard_map/jit(cholesky)/cholesky | solution.py:26
  257.6 6.1 %custom-call.14 = f32[1,80,80]{1,2,0:T(8,128)S(1)} custom-call(f32[1,80,80]{2,1,0:T(8,128)S(1)} %get-tuple-element.19), custom_call_target="InvertDiagBlocksLowerTriangular" | custom-call | tf_op jit(solution)/shard_map/jit(_solve_triangular)/triangular_solve | solution.py:16
  264.4 16.5 %all_gather.28 = f32[128,1024]{1,0:T(8,128)S(1)} all-gather(f32[8,1024]{1,0:T(8,128)S(1)} %reshape.109), channel_id=1, replica_groups=mesh['row'=16,'col'=16] {'col'}, dimensions={0}, use_global_device_ids=true | all-gather | bytes 557056 | tf_op jit(solution)/shard_map/all_gather | solution.py:58
  280.9 4.4 collective-permute-start.8
  286.9 4.5 collective-permute-done.8
  291.4 2.8 collective-permute-done.9
  295.5 2.2 gather_fusion.4
  305.0 18.8 %all_gather.29 = f32[128,1024]{1,0:T(8,128)S(1)} all-gather(f32[8,1024]{1,0:T(8,128)S(1)} %reshape.111), channel_id=1, replica_groups=mesh['row'=16,'col'=16] {'col'}, dimensions={0}, use_global_device_ids=true | all-gather | bytes 557056 | tf_op jit(solution)/shard_map/all_gather | solution.py:58
  323.9 4.9 collective-permute-start.10
  328.8 2.8 collective-permute-start.11
  331.6 3.3 collective-permute-done.10
  334.9 2.8 collective-permute-done.11
  339.0 2.2 gather_fusion.5
  348.6 15.9 %all_gather.30 = f32[128,1024]{1,0:T(8,128)S(1)} all-gather(f32[8,1024]{1,0:T(8,128)S(1)} %reshape.113), channel_id=1, replica_groups=mesh['row'=16,'col'=16] {'col'}, dimensions={0}, use_global_device_ids=true | all-gather | bytes 557056 | tf_op jit(solution)/shard_map/all_gather | solution.py:58
  364.5 5.2 collective-permute-start.12
  369.7 4.1 collective-permute-start.13
  375.8 2.8 collective-permute-done.13
  379.9 2.2 gather_fusion.6
  390.7 18.5 %all_gather.31 = f32[128,1024]{1,0:T(8,128)S(1)} all-gather(f32[8,1024]{1,0:T(8,128)} %reshape.115), channel_id=1, replica_groups=mesh['row'=16,'col'=16] {'col'}, dimensions={0}, use_global_device_ids=true | all-gather | bytes 557056 | tf_op jit(solution)/shard_map/all_gather | solution.py:58
  409.2 5.5 collective-permute-start.14
  414.7 4.8 collective-permute-start.15
  421.0 2.7 collective-permute-done.15
  423.7 2.5 pad_maximum_fusion.7
  436.4 80.9 %psum.22 = f32[80,64]{0,1:T(8,128)S(1)} all-reduce(f32[80,64]{0,1:T(8,128)S(1)} %convolution_bitcast_fusion.7), channel_id=1, replica_groups=mesh['row'=16,'col'=16] {'row','col'}, use_global_device_ids=true, to_apply=%region_4.6 | all-reduce | flops 5120 | bytes 40960 | tf_op jit(solution)/shard_map/psum | solution.py:90
  518.5 72.7 %psum.23 = f32[64,64]{0,1:T(8,128)S(1)} all-reduce(f32[64,64]{0,1:T(8,128)S(1)} %convolution_bitcast_fusion.6), channel_id=1, replica_groups=mesh['row'=16,'col'=16] {'row','col'}, use_global_device_ids=true, to_apply=%region_5.7 | all-reduce | flops 4096 | bytes 32768 | tf_op jit(solution)/shard_map/psum | solution.py:25
  591.3 5.8 cholesky.65
  598.5 4.9 custom-call.15
  (157 shorter events, 81.2 us)
Async XLA Ops:
  0.6 44.1 %copy-start = (f32[8,64,64]{2,1,0:T(8,128)S(1)}, f32[8,64,64]{2,1,0:T(8,128)}, u32[]{:S(2)}) copy-start(f32[8,64,64]{2,1,0:T(8,128)} %param.9) | copy-start | bytes 393220
  20.7 13.5 %collective-permute-start = (f32[128,1024]{1,0:T(8,128)S(1)}, f32[128,1024]{1,0:T(8,128)}, u32[]{:S(2)}, u32[]{:S(2)}) collective-permute-start(f32[128,1024]{1,0:T(8,128)S(1)} %all_gather.24), channel_id=1, source_target_pairs={{0,16},{16,32},{32,48},{48,64},{64,80},{80,96},{96,112},{112,128},... | collective-permute-start | bytes 1572872 | tf_op jit(solution)/shard_map/ppermute | solution.py:11
  28.1 8.7 %collective-permute-start.1 = (f32[128,1024]{1,0:T(8,128)S(1)}, f32[128,1024]{1,0:T(8,128)}, u32[]{:S(2)}, u32[]{:S(2)}) collective-permute-start(f32[128,1024]{1,0:T(8,128)S(1)} %all_gather.24), channel_id=1, source_target_pairs={{0,240},{16,0},{32,16},{48,32},{64,48},{80,64},{96,80},{112,96},{1... | collective-permute-start | bytes 1572872 | tf_op jit(solution)/shard_map/ppermute | solution.py:11
  31.2 1.9 copy-start.18
  42.1 2.7 copy-start.15
  45.9 32.3 %copy-start.11 = (f32[8,16,64]{2,1,0:T(8,128)}, f32[8,16,64]{2,1,0:T(8,128)S(1)}, u32[]{:S(2)}) copy-start(f32[8,16,64]{2,1,0:T(8,128)S(1)} %get-tuple-element.23) | copy-start | bytes 98308
  64.3 11.2 %collective-permute-start.2 = (f32[128,1024]{1,0:T(8,128)S(1)}, f32[128,1024]{1,0:T(8,128)S(1)}, u32[]{:S(2)}, u32[]{:S(2)}) collective-permute-start(f32[128,1024]{1,0:T(8,128)S(1)} %all_gather.25), channel_id=1, source_target_pairs={{0,16},{16,32},{32,48},{48,64},{64,80},{80,96},{96,112},{112,128},... | collective-permute-start | bytes 1572872 | tf_op jit(solution)/shard_map/ppermute | solution.py:11
  69.4 8.9 %collective-permute-start.3 = (f32[128,1024]{1,0:T(8,128)S(1)}, f32[128,1024]{1,0:T(8,128)S(1)}, u32[]{:S(2)}, u32[]{:S(2)}) collective-permute-start(f32[128,1024]{1,0:T(8,128)S(1)} %all_gather.25), channel_id=1, source_target_pairs={{0,240},{16,0},{32,16},{48,32},{64,48},{80,64},{96,80},{112,96},{1... | collective-permute-start | bytes 1572872 | tf_op jit(solution)/shard_map/ppermute | solution.py:11
  83.5 1.4 copy-start.12
  86.2 31.0 %copy-start.13 = (f32[8,16,64]{2,1,0:T(8,128)}, f32[8,16,64]{2,1,0:T(8,128)S(1)}, u32[]{:S(2)}) copy-start(f32[8,16,64]{2,1,0:T(8,128)S(1)} %get-tuple-element.25) | copy-start | bytes 98308
  103.2 11.2 %collective-permute-start.4 = (f32[128,1024]{1,0:T(8,128)S(1)}, f32[128,1024]{1,0:T(8,128)S(1)}, u32[]{:S(2)}, u32[]{:S(2)}) collective-permute-start(f32[128,1024]{1,0:T(8,128)S(1)} %all_gather.26), channel_id=1, source_target_pairs={{0,16},{16,32},{32,48},{48,64},{64,80},{80,96},{96,112},{112,128},... | collective-permute-start | bytes 1572872 | tf_op jit(solution)/shard_map/ppermute | solution.py:11
  108.2 8.9 %collective-permute-start.5 = (f32[128,1024]{1,0:T(8,128)S(1)}, f32[128,1024]{1,0:T(8,128)S(1)}, u32[]{:S(2)}, u32[]{:S(2)}) collective-permute-start(f32[128,1024]{1,0:T(8,128)S(1)} %all_gather.26), channel_id=1, source_target_pairs={{0,240},{16,0},{32,16},{48,32},{64,48},{80,64},{96,80},{112,96},{1... | collective-permute-start | bytes 1572872 | tf_op jit(solution)/shard_map/ppermute | solution.py:11
  122.4 1.4 copy-start.14
  125.0 32.0 %copy-start.9 = (f32[8,16,64]{2,1,0:T(8,128)}, f32[8,16,64]{2,1,0:T(8,128)S(1)}, u32[]{:S(2)}) copy-start(f32[8,16,64]{2,1,0:T(8,128)S(1)} %get-tuple-element.27) | copy-start | bytes 98308
  143.2 11.0 %collective-permute-start.6 = (f32[128,1024]{1,0:T(8,128)S(1)}, f32[128,1024]{1,0:T(8,128)S(1)}, u32[]{:S(2)}, u32[]{:S(2)}) collective-permute-start(f32[128,1024]{1,0:T(8,128)S(1)} %all_gather.27), channel_id=1, source_target_pairs={{0,16},{16,32},{32,48},{48,64},{64,80},{80,96},{96,112},{112,128},... | collective-permute-start | bytes 1572872 | tf_op jit(solution)/shard_map/ppermute | solution.py:11
  148.1 8.9 %collective-permute-start.7 = (f32[128,1024]{1,0:T(8,128)S(1)}, f32[128,1024]{1,0:T(8,128)S(1)}, u32[]{:S(2)}, u32[]{:S(2)}) collective-permute-start(f32[128,1024]{1,0:T(8,128)S(1)} %all_gather.27), channel_id=1, source_target_pairs={{0,240},{16,0},{32,16},{48,32},{64,48},{80,64},{96,80},{112,96},{1... | collective-permute-start | bytes 1572872 | tf_op jit(solution)/shard_map/ppermute | solution.py:11
  162.2 1.4 copy-start.10
  280.9 10.5 %collective-permute-start.8 = (f32[128,1024]{1,0:T(8,128)S(1)}, f32[128,1024]{1,0:T(8,128)S(1)}, u32[]{:S(2)}, u32[]{:S(2)}) collective-permute-start(f32[128,1024]{1,0:T(8,128)S(1)} %all_gather.28), channel_id=1, source_target_pairs={{0,16},{16,32},{32,48},{48,64},{64,80},{80,96},{96,112},{112,128},... | collective-permute-start | bytes 1572872 | tf_op jit(solution)/shard_map/ppermute | solution.py:11
  285.3 8.9 %collective-permute-start.9 = (f32[128,1024]{1,0:T(8,128)S(1)}, f32[128,1024]{1,0:T(8,128)S(1)}, u32[]{:S(2)}, u32[]{:S(2)}) collective-permute-start(f32[128,1024]{1,0:T(8,128)S(1)} %all_gather.28), channel_id=1, source_target_pairs={{0,240},{16,0},{32,16},{48,32},{64,48},{80,64},{96,80},{112,96},{1... | collective-permute-start | bytes 1572872 | tf_op jit(solution)/shard_map/ppermute | solution.py:11
  304.9 32.8 %copy-start.1 = (f32[8,16,64]{2,1,0:T(8,128)}, f32[8,16,64]{2,1,0:T(8,128)S(1)}, u32[]{:S(2)}) copy-start(f32[8,16,64]{2,1,0:T(8,128)S(1)} %convolution_add_fusion.3) | copy-start | bytes 98308
  323.9 11.1 %collective-permute-start.10 = (f32[128,1024]{1,0:T(8,128)S(1)}, f32[128,1024]{1,0:T(8,128)S(1)}, u32[]{:S(2)}, u32[]{:S(2)}) collective-permute-start(f32[128,1024]{1,0:T(8,128)S(1)} %all_gather.29), channel_id=1, source_target_pairs={{0,16},{16,32},{32,48},{48,64},{64,80},{80,96},{96,112},{112,128},... | collective-permute-start | bytes 1572872 | tf_op jit(solution)/shard_map/ppermute | solution.py:11
  328.8 8.9 %collective-permute-start.11 = (f32[128,1024]{1,0:T(8,128)S(1)}, f32[128,1024]{1,0:T(8,128)S(1)}, u32[]{:S(2)}, u32[]{:S(2)}) collective-permute-start(f32[128,1024]{1,0:T(8,128)S(1)} %all_gather.29), channel_id=1, source_target_pairs={{0,240},{16,0},{32,16},{48,32},{64,48},{80,64},{96,80},{112,96},{1... | collective-permute-start | bytes 1572872 | tf_op jit(solution)/shard_map/ppermute | solution.py:11
  346.4 1.4 copy-start.2
  348.5 30.1 %copy-start.4 = (f32[8,16,64]{2,1,0:T(8,128)}, f32[8,16,64]{2,1,0:T(8,128)S(1)}, u32[]{:S(2)}) copy-start(f32[8,16,64]{2,1,0:T(8,128)S(1)} %convolution_add_fusion.2) | copy-start | bytes 98308
  364.5 11.3 %collective-permute-start.12 = (f32[128,1024]{1,0:T(8,128)S(1)}, f32[128,1024]{1,0:T(8,128)S(1)}, u32[]{:S(2)}, u32[]{:S(2)}) collective-permute-start(f32[128,1024]{1,0:T(8,128)S(1)} %all_gather.30), channel_id=1, source_target_pairs={{0,16},{16,32},{32,48},{48,64},{64,80},{80,96},{96,112},{112,128},... | collective-permute-start | bytes 1572872 | tf_op jit(solution)/shard_map/ppermute | solution.py:11
  369.7 8.9 %collective-permute-start.13 = (f32[128,1024]{1,0:T(8,128)S(1)}, f32[128,1024]{1,0:T(8,128)S(1)}, u32[]{:S(2)}, u32[]{:S(2)}) collective-permute-start(f32[128,1024]{1,0:T(8,128)S(1)} %all_gather.30), channel_id=1, source_target_pairs={{0,240},{16,0},{32,16},{48,32},{64,48},{80,64},{96,80},{112,96},{1... | collective-permute-start | bytes 1572872 | tf_op jit(solution)/shard_map/ppermute | solution.py:11
  387.3 1.5 copy-start.5
  388.8 31.5 %copy-start.16 = (f32[80,80]{0,1:T(8,128)S(1)}, f32[80,80]{0,1:T(8,128)}, u32[]{:S(2)}) copy-start(f32[80,80]{0,1:T(8,128)} %get-tuple-element.18) | copy-start | bytes 76804
  389.4 0.6 copy-start.7
  409.2 11.7 %collective-permute-start.14 = (f32[128,1024]{1,0:T(8,128)S(1)}, f32[128,1024]{1,0:T(8,128)}, u32[]{:S(2)}, u32[]{:S(2)}) collective-permute-start(f32[128,1024]{1,0:T(8,128)S(1)} %all_gather.31), channel_id=1, source_target_pairs={{0,16},{16,32},{32,48},{48,64},{64,80},{80,96},{96,112},{112,128},... | collective-permute-start | bytes 1572872 | tf_op jit(solution)/shard_map/ppermute | solution.py:11
  414.7 9.0 %collective-permute-start.15 = (f32[128,1024]{1,0:T(8,128)S(1)}, f32[128,1024]{1,0:T(8,128)}, u32[]{:S(2)}, u32[]{:S(2)}) collective-permute-start(f32[128,1024]{1,0:T(8,128)S(1)} %all_gather.31), channel_id=1, source_target_pairs={{0,240},{16,0},{32,16},{48,32},{64,48},{80,64},{96,80},{112,96},{1... | collective-permute-start | bytes 1572872 | tf_op jit(solution)/shard_map/ppermute | solution.py:11
  433.7 1.5 copy-start.8
  433.7 2.0 copy-start.3
  433.7 2.0 copy-start.6
  517.3 87.7 %copy-start.17 = (f32[80,64]{0,1:T(8,128)}, f32[80,64]{0,1:T(8,128)S(1)}, u32[]{:S(2)}) copy-start(f32[80,64]{0,1:T(8,128)S(1)} %broadcast_multiply_fusion.2) | copy-start | bytes 61444
where the time goes:
time: 614 us; the launch traced here: 606 us
  blocking collectives  379 us (62%)
  starting transfers between devices  58.2 us (9%)
  waiting for transfers between devices  48 us (8%)
  other arithmetic  46 us (7%)
  local copies, waits for them, and re-layouts  41.9 us (7%)
  matrix products  31.5 us (5%)
    psum x2, blocking collectives, factor_panel(): gram_all = lax.psum(local_gram, ('row', 'col')) / total_rows  155 us
    all_gather x8, blocking collectives, apply_matrix(): own_group = lax.all_gather(vector, 'col', axis=0, tiled=True)  143 us
    psum x1, blocking collectives, per_device(): coupling = lax.psum(local_coupling, ('row', 'col')) / total_rows  80.9 us
    ppermute x16, starting transfers between devices, from_behind(): return lax.ppermute(x, axis, [(i, (i + by) % peers) for i in range(peers)])  58.2 us
    ppermute x16, waiting for transfers between devices, from_behind(): return lax.ppermute(x, axis, [(i, (i + by) % peers) for i in range(peers)])  48 us
    gather x16, local copies, waits for them, and re-layouts, apply_matrix(): jnp.take(whole, slot_pos, axis=0)  21.5 us
    another operation x6, other arithmetic, factor_panel(): lower = jnp.linalg.cholesky(gram_all)  14.5 us
    concatenate x8, other arithmetic, apply_matrix(): whole = jnp.concatenate([own_group, prev_group, next_group], 0)  12.7 us
  transfers between devices with their start and end apart: 16, of which 15 were waited for; matrix products, arithmetic and copies ran while one was open for 1% of the time, Pallas kernels for 0%

commit v1 on v0

v1 whole, which is shorter than its diff:
```python
import functools

import jax
import jax.numpy as jnp
from jax import lax
from jax.experimental import pallas as pl
from jax.experimental.pallas import tpu as pltpu
from jax.sharding import PartitionSpec as P

MESH = pl.DeviceIdType.MESH
HIGHEST = lax.Precision.HIGHEST
STEPS = 4
POWERS = 2 * STEPS
BS = 64
RHS = 16
SLOTS = 9
OWN = 8
COLS = 16
ROWS_AXIS = 16
GROUP = OWN * COLS
PANEL = (STEPS + 1) * RHS
NEW = STEPS * RHS
ALL = (POWERS + 1) * RHS
WIDE = OWN * BS
SCALE = 1.0 / (GROUP * ROWS_AXIS * BS)


def dot(a, b, contract):
    return lax.dot_general(
        a, b, (contract, ((), ())), precision=HIGHEST, preferred_element_type=jnp.float32
    )


def nt(a, b):
    return dot(a, b, ((1,), (1,)))


def nn(a, b):
    return dot(a, b, ((1,), (0,)))


def tn(a, b):
    return dot(a, b, ((0,), (0,)))


def local_row(index):
    return lax.rem(index, GROUP)


def side_by_side(a, b):
    low = lax.broadcasted_iota(jnp.int32, a.shape, 1) < BS
    top = jnp.where(low, a, pltpu.roll(b, BS, 1))
    bottom = jnp.where(low, pltpu.roll(a, BS, 1), b)
    return jnp.concatenate([top, bottom], 0)


def factor(gram):
    n = gram.shape[0]
    shape = (n, n)
    sub = lax.broadcasted_iota(jnp.int32, shape, 0)
    lane = lax.broadcasted_iota(jnp.int32, shape, 1)
    lane_row = lax.broadcasted_iota(jnp.int32, (1, n), 1)
    sub_col = lax.broadcasted_iota(jnp.int32, (n, 1), 0)

    def step(k, state):
        left, right = state
        here = sub == k
        row_left = jnp.sum(jnp.where(here, left, 0.0), 0, keepdims=True)
        row_right = jnp.sum(jnp.where(here, right, 0.0), 0, keepdims=True)
        column = jnp.sum(jnp.where(lane == k, left, 0.0), 1, keepdims=True)
        pivot = jnp.sum(jnp.where(lane_row == k, row_left, 0.0), 1, keepdims=True)
        gain = jnp.where(sub_col > k, column / pivot, 0.0)
        return left - gain * row_left, right - gain * row_right

    eye = jnp.where(sub == lane, 1.0, 0.0)
    left, right = lax.fori_loop(0, n, step, (gram, eye))
    pivots = jnp.sum(jnp.where(sub == lane, left, 0.0), 1, keepdims=True)
    scale = lax.rsqrt(pivots)
    scale = scale * (1.5 - 0.5 * pivots * scale * scale)
    return jnp.where(lane >= sub, left, 0.0) * scale, right * scale


def kernel(
    start_ref, stiff_ref, convect_ref, index_ref, index_vmem, upwind_ref,
    first_ref, second_ref, factor_first_ref, coupling_ref, factor_second_ref,
    field, rows_prev, rows_next, give, w_main, w_far, partial, powers, w_all,
    index_in, index_next, index_prev,
    sum_in, sum_a, sum_b, sum_out,
    send_sem, recv_sem, far_send, far_recv, index_send, index_recv, index_local,
    sum_send, sum_recv,
):
    row = lax.axis_index("row")
    col = lax.axis_index("col")
    sector_peers = [(row, lax.rem(col + i, COLS)) for i in range(1, COLS)]
    row_peers = [(lax.rem(row + i, ROWS_AXIS), col) for i in range(1, ROWS_AXIS)]
    nxt, prv = row_peers[0], row_peers[-1]

    barrier = pltpu.get_barrier_semaphore()
    for peer in sector_peers + row_peers:
        pl.semaphore_signal(barrier, inc=1, device_id=peer, device_id_type=MESH)
    own = pl.ds(col * OWN, OWN)
    field[0][own] = start_ref[...]
    pl.semaphore_wait(barrier, COLS + ROWS_AXIS - 2)

    pending = []

    def push(src, dst, send, recv, peer):
        copy = pltpu.make_async_remote_copy(
            src_ref=src, dst_ref=dst, send_sem=send, recv_sem=recv, device_id=peer, device_id_type=MESH
        )
        copy.start()
        pending.append(copy)
        return copy

    def arrived(ref, sem):
        pltpu.make_async_copy(ref, ref, sem).wait()

    def spread(t):
        mine = field[t].at[own]
        for i, peer in enumerate(sector_peers):
            push(mine, mine, send_sem.at[t, i], recv_sem.at[t, col], peer)

    def gathered(t):
        for i in range(1, COLS):
            other = lax.rem(col + i, COLS)
            arrived(field[t].at[pl.ds(other * OWN, OWN)], recv_sem.at[t, other])

    def keep(t, rows):
        for b in range(0, OWN, 2):
            powers[t * RHS : (t + 1) * RHS, b * BS : (b + 2) * BS] = rows(b)

    def sum_first(s, tiles):
        for i in range(tiles):
            @pl.when(col != i)
            def _(i=i):
                copy = pltpu.make_async_remote_copy(
                    src_ref=sum_in[s].at[i], dst_ref=sum_a[s].at[col], send_sem=sum_send.at[s, 0, i],
                    recv_sem=sum_recv.at[s, 0, col], device_id=(row, i), device_id_type=MESH,
                )
                copy.start()

    def sum_second(s, tiles):
        for i in range(tiles):
            @pl.when(col != i)
            def _(i=i):
                pltpu.make_async_copy(sum_in[s].at[i], sum_in[s].at[i], sum_send.at[s, 0, i]).wait()

        @pl.when(col < tiles)
        def _():
            sum_a[s][col] = sum_in[s][col]
            for i in range(1, COLS):
                other = lax.rem(col + i, COLS)
                arrived(sum_a[s].at[other], sum_recv.at[s, 0, other])
            total = sum_a[s][0]
            for i in range(1, COLS):
                total = total + sum_a[s][i]
            sum_b[s][row] = total
            for i, peer in enumerate(row_peers):
                pltpu.make_async_remote_copy(
                    src_ref=sum_b[s].at[row], dst_ref=sum_b[s].at[row], send_sem=sum_send.at[s, 1, i],
                    recv_sem=sum_recv.at[s, 1, row], device_id=peer, device_id_type=MESH,
                ).start()

    def sum_third(s, tiles):
        @pl.when(col < tiles)
        def _():
            for i in range(1, ROWS_AXIS):
                other = lax.rem(row + i, ROWS_AXIS)
                arrived(sum_b[s].at[other], sum_recv.at[s, 1, other])
            for i in range(ROWS_AXIS - 1):
                pltpu.make_async_copy(sum_b[s].at[row], sum_b[s].at[row], sum_send.at[s, 1, i]).wait()
            total = sum_b[s][0]
            for i in range(1, ROWS_AXIS):
                total = total + sum_b[s][i]
            sum_out[s][col] = total
            for i, peer in enumerate(sector_peers):
                pltpu.make_async_remote_copy(
                    src_ref=sum_out[s].at[col], dst_ref=sum_out[s].at[col], send_sem=sum_send.at[s, 2, i],
                    recv_sem=sum_recv.at[s, 2, col], device_id=peer, device_id_type=MESH,
                ).start()

    def sum_end(s, tiles):
        for i in range(tiles):
            @pl.when(col != i)
            def _(i=i):
                arrived(sum_out[s].at[i], sum_recv.at[s, 2, i])

        @pl.when(col < tiles)
        def _():
            for i in range(COLS - 1):
                pltpu.make_async_copy(sum_out[s].at[col], sum_out[s].at[col], sum_send.at[s, 2, i]).wait()

    spread(0)
    push(index_vmem, index_in.at[0], index_send.at[0], index_recv.at[0], nxt)
    push(index_vmem, index_in.at[1], index_send.at[1], index_recv.at[1], prv)
    keep(0, lambda b: side_by_side(start_ref[b], start_ref[b + 1]))

    zero = jnp.zeros((BS, BS), jnp.float32)
    for b in range(OWN):
        flags = [upwind_ref[b, j].astype(jnp.float32) for j in range(SLOTS)]
        total = functools.reduce(lambda x, y: x + y, flags)
        flags[0] = flags[0] - total
        convect = convect_ref[b]
        blocks = [stiff_ref[b, :, j * BS : (j + 1) * BS] + flags[j] * convect for j in range(SLOTS)]
        for j in range(0, 6, 2):
            w_main[b, :, j * BS : (j + 2) * BS] = jnp.concatenate(blocks[j : j + 2], 1)
        w_main[b, :, 6 * BS : 8 * BS] = jnp.concatenate([blocks[6], zero], 1)
        w_far[b] = jnp.concatenate(blocks[7:9], 1)

    arrived(index_in.at[0], index_recv.at[0])
    arrived(index_in.at[1], index_recv.at[1])
    local = [
        pltpu.make_async_copy(index_in.at[0], index_prev, index_local.at[0]),
        pltpu.make_async_copy(index_in.at[1], index_next, index_local.at[1]),
    ]
    for copy in local:
        copy.start()
    for copy in local:
        copy.wait()

    def apply(t):
        f = field[t]
        gathered(t)
        for b in range(OWN):
            give[t][0, b] = f[local_row(index_next[b, SLOTS - 2])]
            give[t][1, b] = f[local_row(index_prev[b, SLOTS - 1])]
        push(give[t].at[0], rows_prev[t], far_send.at[t, 0], far_recv.at[t, 0], nxt)
        push(give[t].at[1], rows_next[t], far_send.at[t, 1], far_recv.at[t, 1], prv)
        for b in range(OWN):
            tiles = [f[col * OWN + b]] + [f[local_row(index_ref[b, j])] for j in range(1, 7)]
            tiles.append(jnp.zeros_like(tiles[0]))
            near = jnp.concatenate([side_by_side(tiles[j], tiles[j + 1]) for j in range(0, 8, 2)], 1)
            partial[b] = nt(near, w_main[b])
        arrived(rows_prev[t], far_recv.at[t, 0])
        arrived(rows_next[t], far_recv.at[t, 1])
        results = []
        for b in range(OWN):
            near = side_by_side(rows_prev[t][b], rows_next[t][b])
            result = partial[b] + nt(near, w_far[b])
            results.append(result)
            if t + 1 < POWERS:
                field[t + 1][col * OWN + b] = jnp.concatenate([result[:8], result[8:]], 1)
        if t + 1 < POWERS:
            spread(t + 1)
        keep(t + 1, lambda b: jnp.concatenate([results[b], results[b + 1]], 1))

    for t in range(STEPS):
        apply(t)

    tiles_one = PANEL // 8
    panel = powers[:PANEL, :]
    gram = nt(panel, panel)
    wide = jnp.concatenate([gram, jnp.zeros((PANEL, 128 - PANEL), jnp.float32)], 1)
    for i in range(tiles_one):
        sum_in[0][i] = wide[i * 8 : (i + 1) * 8]
    sum_first(0, tiles_one)
    apply(STEPS)
    sum_second(0, tiles_one)
    apply(STEPS + 1)
    sum_third(0, tiles_one)
    apply(STEPS + 2)
    sum_end(0, tiles_one)
    gram = jnp.concatenate([sum_out[0][i] for i in range(tiles_one)], 0)[:, :PANEL] * SCALE
    upper_one, inverse_one = factor(gram)
    factor_first_ref[...] = upper_one
    first = nn(inverse_one, powers[:PANEL, :])
    first_ref[...] = first
    mix = inverse_one[PANEL - RHS :]
    for k in range(1, STEPS):
        w_all[(k - 1) * RHS : k * RHS] = nn(mix, powers[k * RHS : k * RHS + PANEL])
    apply(STEPS + 3)
    w_all[NEW - RHS :] = nn(mix, powers[STEPS * RHS :])

    fresh = w_all[...]
    first = first_ref[...]
    cross = nt(first, fresh)
    square = nt(fresh, fresh)
    both = jnp.concatenate([cross, square], 0)
    half = (PANEL + NEW) // 2
    tiles_two = half // 8
    wide = jnp.concatenate([both[:half], both[half:]], 1)
    for i in range(tiles_two):
        sum_in[1][i] = wide[i * 8 : (i + 1) * 8]
    sum_first(1, tiles_two)
    sum_second(1, tiles_two)
    sum_third(1, tiles_two)
    sum_end(1, tiles_two)
    wide = jnp.concatenate([sum_out[1][i] for i in range(tiles_two)], 0) * SCALE
    coupling = jnp.concatenate([wide[:, :NEW], wide[: PANEL - half, NEW:]], 0)
    square = wide[PANEL - half :, NEW:]
    coupling_ref[...] = coupling
    gram = square - tn(coupling, coupling)
    upper_two, inverse_two = factor(gram)
    factor_second_ref[...] = upper_two
    projected = fresh - tn(coupling, first)
    second_ref[...] = nn(inverse_two, projected)

    for copy in pending:
        copy.wait_send()


def per_device(start, stiff, convect, column_index, upwind):
    tiles = start.reshape(OWN, 2, 8, BS).transpose(0, 2, 1, 3).reshape(OWN, 8, 2 * BS)
    vmem = pl.BlockSpec(memory_space=pltpu.VMEM)
    smem = pl.BlockSpec(memory_space=pltpu.SMEM)
    f32 = jnp.float32
    rows = pltpu.VMEM((OWN, 8, 128), f32)
    sums = lambda: [pltpu.VMEM((16, 8, 128), f32) for _ in range(2)]
    first, second, factor_first, coupling, factor_second = pl.pallas_call(
        kernel,
        out_shape=(
            jax.ShapeDtypeStruct((PANEL, WIDE), f32),
            jax.ShapeDtypeStruct((NEW, WIDE), f32),
            jax.ShapeDtypeStruct((PANEL, PANEL), f32),
            jax.ShapeDtypeStruct((PANEL, NEW), f32),
            jax.ShapeDtypeStruct((NEW, NEW), f32),
        ),
        in_specs=[vmem, vmem, vmem, smem, vmem, smem],
        out_specs=(vmem,) * 5,
        scratch_shapes=[
            [pltpu.VMEM((GROUP, 8, 128), f32) for _ in range(POWERS)],
            [rows for _ in range(POWERS)],
            [rows for _ in range(POWERS)],
            [pltpu.VMEM((2, OWN, 8, 128), f32) for _ in range(POWERS)],
            pltpu.VMEM((OWN, BS, 8 * BS), f32),
            pltpu.VMEM((OWN, BS, 2 * BS), f32),
            pltpu.VMEM((OWN, RHS, BS), f32),
            pltpu.VMEM((ALL, WIDE), f32),
            pltpu.VMEM((NEW, WIDE), f32),
            pltpu.VMEM((2, OWN, SLOTS), jnp.int32),
            pltpu.SMEM((OWN, SLOTS), jnp.int32),
            pltpu.SMEM((OWN, SLOTS), jnp.int32),
            sums(),
            sums(),
            sums(),
            sums(),
            pltpu.SemaphoreType.DMA((POWERS, COLS)),
            pltpu.SemaphoreType.DMA((POWERS, COLS)),
            pltpu.SemaphoreType.DMA((POWERS, 2)),
            pltpu.SemaphoreType.DMA((POWERS, 2)),
            pltpu.SemaphoreType.DMA((2,)),
            pltpu.SemaphoreType.DMA((2,)),
            pltpu.SemaphoreType.DMA((2,)),
            pltpu.SemaphoreType.DMA((2, 3, 16)),
            pltpu.SemaphoreType.DMA((2, 3, 16)),
        ],
        compiler_params=pltpu.CompilerParams(
            collective_id=0, has_side_effects=True, vmem_limit_bytes=40 << 20
        ),
    )(tiles, stiff, convect, column_index, column_index, upwind)
    blocks = lambda basis: basis.reshape(-1, OWN, BS).transpose(1, 0, 2).reshape(OWN, -1)
    return blocks(first), blocks(second), factor_first, coupling, factor_second


def solution(mesh):
    return jax.shard_map(
        per_device,
        mesh=mesh,
        in_specs=(
            P(("row", "col"), None),
            P(("row", "col"), None, None),
            P(("row", "col"), None, None),
            P(("row", "col"), None),
            P(("row", "col"), None),
        ),
        out_specs=(P(("row", "col"), None), P(("row", "col"), None), P(), P(), P()),
        check_vma=False,
    )
```

time: 614 us -> 150 us (0.24); the launches traced: 606 us -> 150 us
  blocking collectives: 379 us -> 0 us
  Pallas kernels: 0 us -> 140 us
  starting transfers between devices: 58.2 us -> 0 us
  waiting for transfers between devices: 48 us -> 0 us
  other arithmetic: 46 us -> 0 us
  local copies, waits for them, and re-layouts: 41.9 us -> 8.45 us
  matrix products: 31.5 us -> 0 us
    psum x3 -> x0, blocking collectives: 235 us -> none  [the longest x2 155 us: factor_panel(): gram_all = lax.psum(local_gram, ('row', 'col')) / total_rows]
    all_gather x8 -> x0, blocking collectives: 143 us -> none  [apply_matrix(): own_group = lax.all_gather(vector, 'col', axis=0, tiled=True)]
    pallas_call x0 -> x1, Pallas kernels: none -> 140 us  [per_device(): pl.pallas_call(kernel, out_shape=(jax.ShapeDtypeStruct((PANEL, WIDE), f32...]
    ppermute x16 -> x0, starting transfers between devices: 58.2 us -> none  [from_behind(): return lax.ppermute(x, axis, [(i, (i + by) % peers) for i in range(peers)])]
    ppermute x16 -> x0, waiting for transfers between devices: 48 us -> none  [from_behind(): return lax.ppermute(x, axis, [(i, (i + by) % peers) for i in range(peers)])]
    dot_general x30 -> x0, matrix products: 31.1 us -> none  [the longest x8 11.4 us: apply_matrix(): jnp.einsum('bijk,bjrk->bri', weights, near, precision=lax.Precision.HIGHEST)]
    another operation x9 -> x0, other arithmetic: 25.5 us -> none  [the longest x6 14.5 us: factor_panel(): lower = jnp.linalg.cholesky(gram_all)]
    gather x16 -> x0, local copies, waits for them, and re-layouts: 21.5 us -> none  [apply_matrix(): jnp.take(whole, slot_pos, axis=0)]
  transfers between devices with their start and end apart: 16 -> 0, of which waited for: 15 -> 0; matrix products, arithmetic and copies ran while one was open for 1% -> 0% of each run, Pallas kernels for 0% -> 0%
where the time goes in v1:
time: 150 us
  Pallas kernels  140 us (93%)
  local copies, waits for them, and re-layouts  8.45 us (6%)
    pallas_call x1, Pallas kernels, per_device(): pl.pallas_call(kernel, out_shape=(jax.ShapeDtypeStruct((PANEL, WIDE), f32...  140 us
    unnamed x11, local copies, waits for them, and re-layouts  5.57 us

profile of v1, /device:TPU:1, one launch (start us, length us, event | category | flops | bytes accessed | tf_op | source)
XLA Modules:
  0.0 149.6 jit_solution(13443295598086725576)
XLA Ops:
  0.6 0.8 reshape.28
  1.5 0.1 reshape.29.start_ref
  1.6 0.0 copy-start
  1.6 1.3 copy-done
  2.9 0.0 copy-start.1
  2.9 0.9 copy-done.1
  3.9 0.0 copy-start.2
  3.9 0.7 copy-done.2
  4.6 0.0 copy-start.3
  4.6 0.7 copy-done.3
  5.2 140.5 %shard_map.92 = (f32[80,512]{1,0:T(8,128)S(1)}, f32[64,512]{1,0:T(8,128)S(1)}, f32[80,80]{1,0:T(8,128)S(1)}, f32[80,64]{1,0:T(8,128)S(1)}, f32[64,64]{1,0:T(8,128)S(1)}) custom-call(f32[8,8,128]{2,1,0:T(8,128)S(1)} %reshape.29.start_ref, f32[8,64,576]{2,1,0:T(8,128)S(1)} %copy-done, f32[8,64,64]{2,1,0:T(8,128)S(1)} %copy-done.1, s32[8,9]{1,0:T(8,128)S(1)} %copy-done.2, ...), custom_call_target="tpu_custom_call" | custom-call | tf_op jit(solution)/shard_map/pallas_call | solution.py:309
  145.7 0.7 copy.17
  146.4 0.1 reshape.30
  146.6 0.1 copy.15
  146.6 0.8 reshape.31
  147.4 0.1 reshape.32
  147.5 0.1 copy.16
  147.6 0.8 reshape.33
  148.4 0.6 copy.22
  149.0 0.6 copy.23
  (1 shorter events, 0.0 us)
Async XLA Ops:
  1.6 1.3 copy-start
  2.9 0.9 copy-start.1
  3.9 0.7 copy-start.2
  4.6 0.7 copy-start.3

commit v2 on v1

--- a/solution.py
+++ b/solution.py
@@ -16,12 +16,15 @@
 SLOTS = 9
 OWN = 8
 COLS = 16
+SIDE = 4
 ROWS_AXIS = 16
 GROUP = OWN * COLS
 PANEL = (STEPS + 1) * RHS
 NEW = STEPS * RHS
 ALL = (POWERS + 1) * RHS
 WIDE = OWN * BS
+HALVES = 2
+PART = RHS // HALVES
 SCALE = 1.0 / (GROUP * ROWS_AXIS * BS)
 
 
@@ -56,50 +59,75 @@
 
 def factor(gram):
     n = gram.shape[0]
-    shape = (n, n)
+    tiles = n // 8
+    shape = (8, n)
     sub = lax.broadcasted_iota(jnp.int32, shape, 0)
     lane = lax.broadcasted_iota(jnp.int32, shape, 1)
-    lane_row = lax.broadcasted_iota(jnp.int32, (1, n), 1)
-    sub_col = lax.broadcasted_iota(jnp.int32, (n, 1), 0)
-
-    def step(k, state):
-        left, right = state
-        here = sub == k
-        row_left = jnp.sum(jnp.where(here, left, 0.0), 0, keepdims=True)
-        row_right = jnp.sum(jnp.where(here, right, 0.0), 0, keepdims=True)
-        column = jnp.sum(jnp.where(lane == k, left, 0.0), 1, keepdims=True)
-        pivot = jnp.sum(jnp.where(lane_row == k, row_left, 0.0), 1, keepdims=True)
-        gain = jnp.where(sub_col > k, column / pivot, 0.0)
-        return left - gain * row_left, right - gain * row_right
-
-    eye = jnp.where(sub == lane, 1.0, 0.0)
-    left, right = lax.fori_loop(0, n, step, (gram, eye))
-    pivots = jnp.sum(jnp.where(sub == lane, left, 0.0), 1, keepdims=True)
-    scale = lax.rsqrt(pivots)
-    scale = scale * (1.5 - 0.5 * pivots * scale * scale)
-    return jnp.where(lane >= sub, left, 0.0) * scale, right * scale
+    left = [gram[8 * i : 8 * i + 8] for i in range(tiles)]
+    right = [jnp.where(lane == sub + 8 * i, 1.0, 0.0) for i in range(tiles)]
+    upper, inverse = [], []
+    for k in range(tiles):
+        columns = [
+            [jnp.broadcast_to(left[i][:, 8 * k + j : 8 * k + j + 1], shape) if i >= k else None for i in range(tiles)]
+            for j in range(8)
+        ]
+        pivots = jnp.ones(shape, jnp.float32)
+        for j in range(8):
+            pivot = columns[j][k][j : j + 1]
+            scale = 1.0 / pivot
+            pivots = jnp.where(sub == j, pivot, pivots)
+            across = [columns[c][k][j : j + 1] for c in range(8)]
+            row_left, row_right = left[k][j : j + 1], right[k][j : j + 1]
+            for i in range(k, tiles):
+                gain = columns[j][i] * scale
+                if i == k:
+                    gain = jnp.where(sub > j, gain, 0.0)
+                for c in range(j + 1, 8):
+                    columns[c][i] = columns[c][i] - gain * across[c]
+                left[i] = left[i] - gain * row_left
+                right[i] = right[i] - gain * row_right
+        scale = lax.rsqrt(pivots)
+        scale = scale * (1.5 - 0.5 * pivots * scale * scale)
+        upper.append(jnp.where(lane >= sub + 8 * k, left[k], 0.0) * scale)
+        inverse.append(right[k] * scale)
+    return jnp.concatenate(upper, 0), jnp.concatenate(inverse, 0)
 
 
 def kernel(
-    start_ref, stiff_ref, convect_ref, index_ref, index_vmem, upwind_ref,
+    start_ref, stiff_hbm, convect_hbm, index_hbm, upwind_hbm,
     first_ref, second_ref, factor_first_ref, coupling_ref, factor_second_ref,
-    field, rows_prev, rows_next, give, w_main, w_far, partial, powers, w_all,
-    index_in, index_next, index_prev,
+    field, rows_prev, rows_next, give, stiff_ref, convect_ref, w_main, w_far, partial, powers, w_all, mix_ref,
+    index_in, index_ref, upwind_ref, index_next, index_prev,
     sum_in, sum_a, sum_b, sum_out,
-    send_sem, recv_sem, far_send, far_recv, index_send, index_recv, index_local,
+    send_sem, recv_sem, far_send, far_recv, index_send, index_recv, local_sem,
     sum_send, sum_recv,
 ):
     row = lax.axis_index("row")
     col = lax.axis_index("col")
-    sector_peers = [(row, lax.rem(col + i, COLS)) for i in range(1, COLS)]
+    away = lambda i: min(i, SIDE - i)
+    steps = sorted(
+        ((i, j) for i in range(SIDE) for j in range(SIDE) if i or j), key=lambda p: -away(p[0]) - away(p[1])
+    )
+    sector_peers = [
+        (row, lax.rem(col // SIDE + i, SIDE) * SIDE + lax.rem(lax.rem(col, SIDE) + j, SIDE)) for i, j in steps
+    ]
     row_peers = [(lax.rem(row + i, ROWS_AXIS), col) for i in range(1, ROWS_AXIS)]
     nxt, prv = row_peers[0], row_peers[-1]
 
     barrier = pltpu.get_barrier_semaphore()
     for peer in sector_peers + row_peers:
         pl.semaphore_signal(barrier, inc=1, device_id=peer, device_id_type=MESH)
+    loads = [
+        pltpu.make_async_copy(src, dst, local_sem.at[i])
+        for i, (src, dst) in enumerate(
+            [(index_hbm, index_ref), (upwind_hbm, upwind_ref), (convect_hbm, convect_ref), (stiff_hbm, stiff_ref)]
+        )
+    ]
+    for copy in loads:
+        copy.start()
     own = pl.ds(col * OWN, OWN)
-    field[0][own] = start_ref[...]
+    for h in range(HALVES):
+        field[0][h][own] = start_ref[h]
     pl.semaphore_wait(barrier, COLS + ROWS_AXIS - 2)
 
     pending = []
@@ -109,25 +137,22 @@
             src_ref=src, dst_ref=dst, send_sem=send, recv_sem=recv, device_id=peer, device_id_type=MESH
         )
         copy.start()
-        pending.append(copy)
         return copy
 
     def arrived(ref, sem):
         pltpu.make_async_copy(ref, ref, sem).wait()
 
-    def spread(t):
-        mine = field[t].at[own]
-        for i, peer in enumerate(sector_peers):
-            push(mine, mine, send_sem.at[t, i], recv_sem.at[t, col], peer)
-
-    def gathered(t):
-        for i in range(1, COLS):
-            other = lax.rem(col + i, COLS)
-            arrived(field[t].at[pl.ds(other * OWN, OWN)], recv_sem.at[t, other])
-
-    def keep(t, rows):
+    def others(t, h):
+        return field[t][h].at[pl.ds(0, GROUP - OWN)]
+
+    def spread(t, h):
+        mine = field[t][h].at[own]
+        for peer in sector_peers:
+            push(mine, mine, send_sem.at[t, h], recv_sem.at[t, h], peer)
+
+    def keep(t, h, rows):
         for b in range(0, OWN, 2):
-            powers[t * RHS : (t + 1) * RHS, b * BS : (b + 2) * BS] = rows(b)
+            powers[t * RHS + h * PART : t * RHS + (h + 1) * PART, b * BS : (b + 2) * BS] = rows(b)
 
     def sum_first(s, tiles):
         for i in range(tiles):
@@ -190,11 +215,15 @@
             for i in range(COLS - 1):
                 pltpu.make_async_copy(sum_out[s].at[col], sum_out[s].at[col], sum_send.at[s, 2, i]).wait()
 
-    spread(0)
-    push(index_vmem, index_in.at[0], index_send.at[0], index_recv.at[0], nxt)
-    push(index_vmem, index_in.at[1], index_send.at[1], index_recv.at[1], prv)
-    keep(0, lambda b: side_by_side(start_ref[b], start_ref[b + 1]))
-
+    for h in range(HALVES):
+        spread(0, h)
+    pending.append(push(index_hbm, index_in.at[0], index_send.at[0], index_recv.at[0], nxt))
+    pending.append(push(index_hbm, index_in.at[1], index_send.at[1], index_recv.at[1], prv))
+    for h in range(HALVES):
+        keep(0, h, lambda b: side_by_side(start_ref[h, b], start_ref[h, b + 1]))
+
+    for copy in loads:
+        copy.wait()
     zero = jnp.zeros((BS, BS), jnp.float32)
     for b in range(OWN):
         flags = [upwind_ref[b, j].astype(jnp.float32) for j in range(SLOTS)]
@@ -210,66 +239,75 @@
     arrived(index_in.at[0], index_recv.at[0])
     arrived(index_in.at[1], index_recv.at[1])
     local = [
-        pltpu.make_async_copy(index_in.at[0], index_prev, index_local.at[0]),
-        pltpu.make_async_copy(index_in.at[1], index_next, index_local.at[1]),
+        pltpu.make_async_copy(index_in.at[0], index_prev, local_sem.at[4]),
+        pltpu.make_async_copy(index_in.at[1], index_next, local_sem.at[5]),
     ]
     for copy in local:
         copy.start()
     for copy in local:
         copy.wait()
 
-    def apply(t):
-        f = field[t]
-        gathered(t)
+    def apply(t, h, beside=()):
+        f = field[t][h]
+        arrived(others(t, h), recv_sem.at[t, h])
         for b in range(OWN):
-            give[t][0, b] = f[local_row(index_next[b, SLOTS - 2])]
-            give[t][1, b] = f[local_row(index_prev[b, SLOTS - 1])]
-        push(give[t].at[0], rows_prev[t], far_send.at[t, 0], far_recv.at[t, 0], nxt)
-        push(give[t].at[1], rows_next[t], far_send.at[t, 1], far_recv.at[t, 1], prv)
+            give[t][h][0, b] = f[local_row(index_next[b, SLOTS - 2])]
+            give[t][h][1, b] = f[local_row(index_prev[b, SLOTS - 1])]
+        pending.append(push(give[t][h].at[0], rows_prev[t].at[h], far_send.at[t, h, 0], far_recv.at[t, h, 0], nxt))
+        pending.append(push(give[t][h].at[1], rows_next[t].at[h], far_send.at[t, h, 1], far_recv.at[t, h, 1], prv))
         for b in range(OWN):
             tiles = [f[col * OWN + b]] + [f[local_row(index_ref[b, j])] for j in range(1, 7)]
             tiles.append(jnp.zeros_like(tiles[0]))
             near = jnp.concatenate([side_by_side(tiles[j], tiles[j + 1]) for j in range(0, 8, 2)], 1)
             partial[b] = nt(near, w_main[b])
-        arrived(rows_prev[t], far_recv.at[t, 0])
-        arrived(rows_next[t], far_recv.at[t, 1])
+        for call in beside:
+            call()
+        arrived(rows_prev[t].at[h], far_recv.at[t, h, 0])
+        arrived(rows_next[t].at[h], far_recv.at[t, h, 1])
         results = []
         for b in range(OWN):
-            near = side_by_side(rows_prev[t][b], rows_next[t][b])
+            near = side_by_side(rows_prev[t][h, b], rows_next[t][h, b])
             result = partial[b] + nt(near, w_far[b])
             results.append(result)
             if t + 1 < POWERS:
-                field[t + 1][col * OWN + b] = jnp.concatenate([result[:8], result[8:]], 1)
+                field[t + 1][h][col * OWN + b] = jnp.concatenate([result[:4], result[4:]], 1)
         if t + 1 < POWERS:
-            spread(t + 1)
-        keep(t + 1, lambda b: jnp.concatenate([results[b], results[b + 1]], 1))
-
+            spread(t + 1, h)
+        keep(t + 1, h, lambda b: jnp.concatenate([results[b], results[b + 1]], 1))
+
+    def gram_first():
+        panel = powers[:PANEL, :]
+        gram = nt(panel, panel)
+        wide = jnp.concatenate([gram, jnp.zeros((PANEL, 128 - PANEL), jnp.float32)], 1)
+        for i in range(tiles_one):
+            sum_in[0][i] = wide[i * 8 : (i + 1) * 8]
+        sum_first(0, tiles_one)
+
+    def factor_one():
+        sum_end(0, tiles_one)
+        gram = jnp.concatenate([sum_out[0][i] for i in range(tiles_one)], 0)[:, :PANEL] * SCALE
+        upper_one, inverse_one = factor(gram)
+        factor_first_ref[...] = upper_one
+        first_ref[...] = nn(inverse_one, powers[:PANEL, :])
+        mix_ref[...] = inverse_one[PANEL - RHS :]
+
+    def mix_early():
+        for k in range(1, STEPS):
+            w_all[(k - 1) * RHS : k * RHS] = nn(mix_ref[...], powers[k * RHS : k * RHS + PANEL])
+
+    tiles_one = PANEL // 8
     for t in range(STEPS):
-        apply(t)
-
-    tiles_one = PANEL // 8
-    panel = powers[:PANEL, :]
-    gram = nt(panel, panel)
-    wide = jnp.concatenate([gram, jnp.zeros((PANEL, 128 - PANEL), jnp.float32)], 1)
-    for i in range(tiles_one):
-        sum_in[0][i] = wide[i * 8 : (i + 1) * 8]
-    sum_first(0, tiles_one)
-    apply(STEPS)
-    sum_second(0, tiles_one)
-    apply(STEPS + 1)
-    sum_third(0, tiles_one)
-    apply(STEPS + 2)
-    sum_end(0, tiles_one)
-    gram = jnp.concatenate([sum_out[0][i] for i in range(tiles_one)], 0)[:, :PANEL] * SCALE
-    upper_one, inverse_one = factor(gram)
-    factor_first_ref[...] = upper_one
-    first = nn(inverse_one, powers[:PANEL, :])
-    first_ref[...] = first
-    mix = inverse_one[PANEL - RHS :]
-    for k in range(1, STEPS):
-        w_all[(k - 1) * RHS : k * RHS] = nn(mix, powers[k * RHS : k * RHS + PANEL])
-    apply(STEPS + 3)
-    w_all[NEW - RHS :] = nn(mix, powers[STEPS * RHS :])
+        for h in range(HALVES):
+            apply(t, h)
+    apply(4, 0, [gram_first])
+    apply(4, 1, [lambda: sum_second(0, tiles_one)])
+    apply(5, 0, [lambda: sum_third(0, tiles_one)])
+    apply(5, 1)
+    apply(6, 0, [factor_one])
+    apply(6, 1)
+    apply(7, 0, [mix_early])
+    apply(7, 1)
+    w_all[NEW - RHS :] = nn(mix_ref[...], powers[STEPS * RHS :])
 
     fresh = w_all[...]
     first = first_ref[...]
@@ -297,14 +335,17 @@
 
     for copy in pending:
         copy.wait_send()
+    for t in range(POWERS):
+        for h in range(HALVES):
+            arrived(others(t, h), send_sem.at[t, h])
 
 
 def per_device(start, stiff, convect, column_index, upwind):
-    tiles = start.reshape(OWN, 2, 8, BS).transpose(0, 2, 1, 3).reshape(OWN, 8, 2 * BS)
+    tiles = start.reshape(OWN, HALVES, 2, 4, BS).transpose(1, 0, 3, 2, 4).reshape(HALVES, OWN, 4, 2 * BS)
     vmem = pl.BlockSpec(memory_space=pltpu.VMEM)
-    smem = pl.BlockSpec(memory_space=pltpu.SMEM)
+    hbm = pl.BlockSpec(memory_space=pl.ANY)
     f32 = jnp.float32
-    rows = pltpu.VMEM((OWN, 8, 128), f32)
+    rows = pltpu.VMEM((HALVES, OWN, 4, 128), f32)
     sums = lambda: [pltpu.VMEM((16, 8, 128), f32) for _ in range(2)]
     first, second, factor_first, coupling, factor_second = pl.pallas_call(
         kernel,
@@ -315,39 +356,44 @@
             jax.ShapeDtypeStruct((PANEL, NEW), f32),
             jax.ShapeDtypeStruct((NEW, NEW), f32),
         ),
-        in_specs=[vmem, vmem, vmem, smem, vmem, smem],
+        in_specs=[vmem, hbm, hbm, hbm, hbm],
         out_specs=(vmem,) * 5,
         scratch_shapes=[
-            [pltpu.VMEM((GROUP, 8, 128), f32) for _ in range(POWERS)],
+            [[pltpu.VMEM((GROUP, 4, 128), f32) for _ in range(HALVES)] for _ in range(POWERS)],
             [rows for _ in range(POWERS)],
             [rows for _ in range(POWERS)],
-            [pltpu.VMEM((2, OWN, 8, 128), f32) for _ in range(POWERS)],
+            [[pltpu.VMEM((2, OWN, 4, 128), f32) for _ in range(HALVES)] for _ in range(POWERS)],
+            pltpu.VMEM((OWN, BS, SLOTS * BS), f32),
+            pltpu.VMEM((OWN, BS, BS), f32),
             pltpu.VMEM((OWN, BS, 8 * BS), f32),
             pltpu.VMEM((OWN, BS, 2 * BS), f32),
-            pltpu.VMEM((OWN, RHS, BS), f32),
+            pltpu.VMEM((OWN, PART, BS), f32),
             pltpu.VMEM((ALL, WIDE), f32),
             pltpu.VMEM((NEW, WIDE), f32),
+            pltpu.VMEM((RHS, PANEL), f32),
             pltpu.VMEM((2, OWN, SLOTS), jnp.int32),
+            pltpu.SMEM((OWN, SLOTS), jnp.int32),
+            pltpu.SMEM((OWN, SLOTS), jnp.int32),
             pltpu.SMEM((OWN, SLOTS), jnp.int32),
             pltpu.SMEM((OWN, SLOTS), jnp.int32),
             sums(),
             sums(),
             sums(),
             sums(),
-            pltpu.SemaphoreType.DMA((POWERS, COLS)),
-            pltpu.SemaphoreType.DMA((POWERS, COLS)),
-            pltpu.SemaphoreType.DMA((POWERS, 2)),
-            pltpu.SemaphoreType.DMA((POWERS, 2)),
+            pltpu.SemaphoreType.DMA((POWERS, HALVES)),
+            pltpu.SemaphoreType.DMA((POWERS, HALVES)),
+            pltpu.SemaphoreType.DMA((POWERS, HALVES, 2)),
+            pltpu.SemaphoreType.DMA((POWERS, HALVES, 2)),
             pltpu.SemaphoreType.DMA((2,)),
             pltpu.SemaphoreType.DMA((2,)),
-            pltpu.SemaphoreType.DMA((2,)),
+            pltpu.SemaphoreType.DMA((6,)),
             pltpu.SemaphoreType.DMA((2, 3, 16)),
             pltpu.SemaphoreType.DMA((2, 3, 16)),
         ],
         compiler_params=pltpu.CompilerParams(
-            collective_id=0, has_side_effects=True, vmem_limit_bytes=40 << 20
+            collective_id=0, has_side_effects=True, vmem_limit_bytes=56 << 20
         ),
-    )(tiles, stiff, convect, column_index, column_index, upwind)
+    )(tiles, stiff, convect, column_index, upwind)
     blocks = lambda basis: basis.reshape(-1, OWN, BS).transpose(1, 0, 2).reshape(OWN, -1)
     return blocks(first), blocks(second), factor_first, coupling, factor_second
 

time: 150 us -> 115 us (0.77)
  Pallas kernels: 140 us -> 107 us
    pallas_call x1, Pallas kernels: 140 us -> 107 us  [per_device(): pl.pallas_call(kernel, out_shape=(jax.ShapeDtypeStruct((PANEL, WIDE), f32...]
    unnamed x11 -> x9, local copies, waits for them, and re-layouts: 5.57 us -> 2.76 us
where the time goes in v2:
time: 115 us
  Pallas kernels  107 us (93%)
  local copies, waits for them, and re-layouts  7.19 us (6%)
    pallas_call x1, Pallas kernels, per_device(): pl.pallas_call(kernel, out_shape=(jax.ShapeDtypeStruct((PANEL, WIDE), f32...  107 us
    unnamed x9, local copies, waits for them, and re-layouts  2.76 us
    reshape x4, local copies, waits for them, and re-layouts, per_device(): basis.reshape(-1, OWN, BS).transpose(1, 0, 2).reshape(OWN, -1)  2.71 us

profile of v2, /device:TPU:1, one launch (start us, length us, event | category | flops | bytes accessed | tf_op | source)
XLA Modules:
  0.0 115.0 jit_solution(15277501823401951054)
XLA Ops:
  0.6 0.8 reshape.28
  1.5 0.7 reshape.29.start_ref
  2.3 107.1 %shard_map.92 = (f32[80,512]{1,0:T(8,128)}, f32[64,512]{1,0:T(8,128)}, f32[80,80]{1,0:T(8,128)}, f32[80,64]{1,0:T(8,128)}, f32[64,64]{1,0:T(8,128)}) custom-call(f32[2,8,4,128]{3,2,1,0:T(4,128)} %reshape.29.start_ref, f32[8,64,576]{2,1,0:T(8,128)} %stiff_hbm.1, f32[8,64,64]{2,1,0:T(8,128)} %convect_hbm.1, s32[8,9]{1,0:T(8,128)} %index_hbm.1, s32[8,9]{1,0:T(8,128)} %upwind_hbm.1), custom_call_target="tpu_custom_call" | custom-call | tf_op jit(solution)/shard_map/pallas_call | solution.py:350
  109.4 0.0 copy-start
  109.4 1.5 %copy.17 = f32[80,64]{0,1:T(8,128)} copy(f32[80,64]{1,0:T(8,128)} %get-tuple-element.23) | data formatting | bytes 40960
  110.9 1.0 reshape.30
  111.9 0.0 copy-start.1
  111.9 0.0 copy-start.2
  111.9 0.1 copy.15
  112.0 0.8 reshape.31
  112.8 0.0 copy-done
  112.8 0.1 reshape.32
  112.9 0.1 copy.16
  113.0 0.8 reshape.33
  113.8 0.0 copy-done.1
  113.8 0.6 copy.22
  114.4 0.0 copy-done.2
  114.4 0.6 copy.23
  (1 shorter events, 0.0 us)
Async XLA Ops:
  109.4 3.5 %copy-start = (f32[64,512]{1,0:T(8,128)S(1)}, f32[64,512]{1,0:T(8,128)}, u32[]{:S(2)}) copy-start(f32[64,512]{1,0:T(8,128)} %get-tuple-element.11) | copy-start | bytes 393220
  111.9 1.8 %copy-start.1 = (f32[80,80]{1,0:T(8,128)S(1)}, f32[80,80]{1,0:T(8,128)}, u32[]{:S(2)}) copy-start(f32[80,80]{1,0:T(8,128)} %get-tuple-element.32) | copy-start | bytes 76804
  111.9 2.5 %copy-start.2 = (f32[64,64]{1,0:T(8,128)S(1)}, f32[64,64]{1,0:T(8,128)}, u32[]{:S(2)}) copy-start(f32[64,64]{1,0:T(8,128)} %get-tuple-element.34) | copy-start | bytes 49156

commit v3 on v2

v3 whole, which is shorter than its diff:
```python
import functools

import jax
import jax.numpy as jnp
from jax import lax
from jax.experimental import pallas as pl
from jax.experimental.pallas import tpu as pltpu
from jax.sharding import PartitionSpec as P

MESH = pl.DeviceIdType.MESH
HIGHEST = lax.Precision.HIGHEST
STEPS = 4
POWERS = 2 * STEPS
BS = 64
RHS = 16
SLOTS = 9
OWN = 8
COLS = 16
SIDE = 4
ROWS_AXIS = 16
GROUP = OWN * COLS
PANEL = (STEPS + 1) * RHS
NEW = STEPS * RHS
ALL = (POWERS + 1) * RHS
WIDE = OWN * BS
HALVES = 2
PART = RHS // HALVES
SCALE = 1.0 / (GROUP * ROWS_AXIS * BS)


def dot(a, b, contract):
    return lax.dot_general(
        a, b, (contract, ((), ())), precision=HIGHEST, preferred_element_type=jnp.float32
    )


def nt(a, b):
    return dot(a, b, ((1,), (1,)))


def nn(a, b):
    return dot(a, b, ((1,), (0,)))


def tn(a, b):
    return dot(a, b, ((0,), (0,)))


def local_row(index):
    return lax.bitwise_and(index, GROUP - 1)


def side_by_side(a, b):
    low = lax.broadcasted_iota(jnp.int32, a.shape, 1) < BS
    top = jnp.where(low, a, pltpu.roll(b, BS, 1))
    bottom = jnp.where(low, pltpu.roll(a, BS, 1), b)
    return jnp.concatenate([top, bottom], 0)


def factor(gram):
    n = gram.shape[0]
    tiles = n // 8
    shape = (8, n)
    sub = lax.broadcasted_iota(jnp.int32, shape, 0)
    lane = lax.broadcasted_iota(jnp.int32, shape, 1)
    left = [gram[8 * i : 8 * i + 8] for i in range(tiles)]
    right = [jnp.where(lane == sub + 8 * i, 1.0, 0.0) for i in range(tiles)]
    upper, inverse = [], []
    for k in range(tiles):
        columns = [
            [jnp.broadcast_to(left[i][:, 8 * k + j : 8 * k + j + 1], shape) if i >= k else None for i in range(tiles)]
            for j in range(8)
        ]
        pivots = jnp.ones(shape, jnp.float32)
        for j in range(8):
            pivot = columns[j][k][j : j + 1]
            scale = 1.0 / pivot
            pivots = jnp.where(sub == j, pivot, pivots)
            across = [columns[c][k][j : j + 1] for c in range(8)]
            row_left, row_right = left[k][j : j + 1], right[k][j : j + 1]
            for i in range(k, tiles):
                gain = columns[j][i] * scale
                if i == k:
                    gain = jnp.where(sub > j, gain, 0.0)
                for c in range(j + 1, 8):
                    columns[c][i] = columns[c][i] - gain * across[c]
                left[i] = left[i] - gain * row_left
                right[i] = right[i] - gain * row_right
        scale = lax.rsqrt(pivots)
        scale = scale * (1.5 - 0.5 * pivots * scale * scale)
        upper.append(jnp.where(lane >= sub + 8 * k, left[k], 0.0) * scale)
        inverse.append(right[k] * scale)
    return jnp.concatenate(upper, 0), jnp.concatenate(inverse, 0)


def kernel(
    start_ref, stiff_hbm, convect_hbm, index_hbm, upwind_hbm,
    first_ref, second_ref, factor_first_ref, coupling_ref, factor_second_ref,
    field, start_tiles, rows_twin, rows_far, give, stiff_ref, convect_ref, w_main, w_far, partial, powers, basis, mix_ref, both_ref, turn_first, turn_second,
    index_in, index_ref, upwind_ref, index_twin, index_far,
    sum_in, sum_a, sum_b, sum_out,
    send_sem, recv_sem, far_send, far_recv, index_send, index_recv, local_sem,
    sum_send, sum_recv,
):
    row = lax.axis_index("row")
    col = lax.axis_index("col")
    away = lambda i: min(i, SIDE - i)
    steps = sorted(
        ((i, j) for i in range(SIDE) for j in range(SIDE) if i or j), key=lambda p: -away(p[0]) - away(p[1])
    )
    sector_peers = [
        (row, lax.rem(col // SIDE + i, SIDE) * SIDE + lax.rem(lax.rem(col, SIDE) + j, SIDE)) for i, j in steps
    ]
    ring = sorted(range(1, ROWS_AXIS), key=lambda i: -min(i, ROWS_AXIS - i))
    row_peers = [(lax.rem(row + i, ROWS_AXIS), col) for i in ring]
    odd = lax.rem(row, 2)
    twin = (row + 1 - 2 * odd, col)
    far = (lax.rem(row + ROWS_AXIS - 1 + 2 * odd, ROWS_AXIS), col)
    slot_twin, slot_far = SLOTS - 2 + odd, SLOTS - 1 - odd

    barrier = pltpu.get_barrier_semaphore()
    for peer in sector_peers + [twin, far]:
        pl.semaphore_signal(barrier, inc=1, device_id=peer, device_id_type=MESH)
    loads = [
        pltpu.make_async_copy(src, dst, local_sem.at[i])
        for i, (src, dst) in enumerate(
            [(index_hbm, index_ref), (upwind_hbm, upwind_ref), (convect_hbm, convect_ref), (stiff_hbm, stiff_ref)]
        )
    ]
    for copy in loads:
        copy.start()
    own = pl.ds(col * OWN, OWN)
    for h in range(HALVES):
        for m in range(4):
            c = (h * PART + m) * BS
            start_tiles[h, :, m, :] = jnp.concatenate([start_ref[:, c : c + BS], start_ref[:, c + 4 * BS : c + 5 * BS]], 1)
        field[0][h][own] = start_tiles[h]
    pl.semaphore_wait(barrier, COLS + 1)

    pending = []

    def push(src, dst, send, recv, peer):
        copy = pltpu.make_async_remote_copy(
            src_ref=src, dst_ref=dst, send_sem=send, recv_sem=recv, device_id=peer, device_id_type=MESH
        )
        copy.start()
        return copy

    def arrived(ref, sem):
        pltpu.make_async_copy(ref, ref, sem).wait()

    def others(t, h):
        return field[t][h].at[pl.ds(0, GROUP - OWN)]

    def spread(t, h):
        mine = field[t][h].at[own]
        for peer in sector_peers:
            push(mine, mine, send_sem.at[t, h], recv_sem.at[t, h], peer)

    def keep(t, h, rows):
        for b in range(0, OWN, 2):
            powers[t * RHS + h * PART : t * RHS + (h + 1) * PART, b * BS : (b + 2) * BS] = rows(b)

    def sum_first(s, tiles):
        for peer in sector_peers:
            @pl.when(peer[1] < tiles)
            def _(peer=peer):
                push(sum_in[s].at[peer[1]], sum_a[s].at[col], sum_send.at[s, 0], sum_recv.at[s, 0], peer)

    def sum_second(s, tiles):
        @pl.when(col < tiles)
        def _():
            sum_a[s][col] = sum_in[s][col]
            arrived(sum_a[s].at[pl.ds(0, COLS - 1)], sum_recv.at[s, 0])
            sum_b[s][row] = total_of(sum_a[s])
            for peer in row_peers:
                push(sum_b[s].at[row], sum_b[s].at[row], sum_send.at[s, 1], sum_recv.at[s, 1], peer)

    def sum_third(s, tiles):
        @pl.when(col < tiles)
        def _():
            arrived(sum_b[s].at[pl.ds(0, ROWS_AXIS - 1)], sum_recv.at[s, 1])
            sum_out[s][col] = total_of(sum_b[s])
            for peer in sector_peers:
                push(sum_out[s].at[col], sum_out[s].at[col], sum_send.at[s, 2], sum_recv.at[s, 2], peer)

    def sum_end(s, tiles):
        @pl.when(col < tiles)
        def _():
            arrived(sum_out[s].at[pl.ds(0, tiles - 1)], sum_recv.at[s, 2])

        @pl.when(col >= tiles)
        def _():
            arrived(sum_out[s].at[pl.ds(0, tiles)], sum_recv.at[s, 2])

    def sum_sent(s, tiles):
        @pl.when(col < tiles)
        def _():
            arrived(sum_in[s].at[pl.ds(0, tiles - 1)], sum_send.at[s, 0])
            arrived(sum_b[s].at[pl.ds(0, ROWS_AXIS - 1)], sum_send.at[s, 1])
            arrived(sum_out[s].at[pl.ds(0, COLS - 1)], sum_send.at[s, 2])

        @pl.when(col >= tiles)
        def _():
            arrived(sum_in[s].at[pl.ds(0, tiles)], sum_send.at[s, 0])

    def total_of(ref):
        terms = [ref[i] for i in range(16)]
        while len(terms) > 1:
            terms = [terms[i] + terms[i + 1] for i in range(0, len(terms), 2)]
        return terms[0]

    for h in range(HALVES):
        spread(0, h)
    pending.append(push(index_hbm, index_in.at[0], index_send.at[0], index_recv.at[0], twin))
    pending.append(push(index_hbm, index_in.at[1], index_send.at[1], index_recv.at[1], far))
    for h in range(HALVES):
        keep(0, h, lambda b: side_by_side(start_tiles[h, b], start_tiles[h, b + 1]))

    for copy in loads:
        copy.wait()
    for b in range(OWN):
        flags = [upwind_ref[b, j].astype(jnp.float32) for j in range(SLOTS)]
        total = functools.reduce(lambda x, y: x + y, flags)
        flags[0] = flags[0] - total
        convect = convect_ref[b]
        blocks = [stiff_ref[b, :, j * BS : (j + 1) * BS] + flags[j] * convect for j in range(SLOTS)]
        for j in range(0, 6, 2):
            w_main[b, :, j * BS : (j + 2) * BS] = jnp.concatenate(blocks[j : j + 2], 1)
        w_main[b, :, 6 * BS : 8 * BS] = jnp.concatenate([blocks[6], jnp.zeros_like(convect)], 1)
        near_far = [jnp.where(odd == 0, blocks[8], blocks[7]), jnp.where(odd == 0, blocks[7], blocks[8])]
        w_far[b] = jnp.concatenate(near_far, 1)

    arrived(index_in.at[0], index_recv.at[0])
    arrived(index_in.at[1], index_recv.at[1])
    local = [
        pltpu.make_async_copy(index_in.at[0], index_twin, local_sem.at[4]),
        pltpu.make_async_copy(index_in.at[1], index_far, local_sem.at[5]),
    ]
    for copy in local:
        copy.start()
    for copy in local:
        copy.wait()

    def apply(t, h, beside=()):
        f = field[t][h]
        arrived(others(t, h), recv_sem.at[t, h])
        for b in range(OWN):
            give[t][h][0, b] = f[local_row(index_far[b, slot_far])]
        pending.append(push(give[t][h].at[0], rows_far[t].at[h], far_send.at[t, h, 0], far_recv.at[t, h, 0], far))
        for b in range(OWN):
            give[t][h][1, b] = f[local_row(index_twin[b, slot_twin])]
        pending.append(push(give[t][h].at[1], rows_twin[t].at[h], far_send.at[t, h, 1], far_recv.at[t, h, 1], twin))
        for b in range(OWN):
            tiles = [f[col * OWN + b]] + [f[local_row(index_ref[b, j])] for j in range(1, 7)]
            tiles.append(jnp.zeros_like(tiles[0]))
            near = jnp.concatenate([side_by_side(tiles[j], tiles[j + 1]) for j in range(0, 8, 2)], 1)
            partial[b] = nt(near, w_main[b])
        arrived(rows_twin[t].at[h], far_recv.at[t, h, 1])
        for call in beside:
            call()
        arrived(rows_far[t].at[h], far_recv.at[t, h, 0])
        results = []
        for b in range(OWN):
            result = partial[b] + nt(side_by_side(rows_twin[t][h, b], rows_far[t][h, b]), w_far[b])
            results.append(result)
            if t + 1 < POWERS:
                field[t + 1][h][col * OWN + b] = jnp.concatenate([result[:4], result[4:]], 1)
        if t + 1 < POWERS:
            spread(t + 1, h)
        keep(t + 1, h, lambda b: jnp.concatenate([results[b], results[b + 1]], 1))
        arrived(others(t, h), send_sem.at[t, h])
        for copy in pending:
            copy.wait_send()
        pending.clear()

    def gram_first():
        panel = powers[:PANEL, :]
        gram = nt(panel, panel)
        wide = jnp.concatenate([gram, jnp.zeros((PANEL, 128 - PANEL), jnp.float32)], 1)
        for i in range(tiles_one):
            sum_in[0][i] = wide[i * 8 : (i + 1) * 8]
        sum_first(0, tiles_one)

    def factor_one():
        sum_end(0, tiles_one)
        gram = jnp.concatenate([sum_out[0][i] for i in range(tiles_one)], 0)[:, :PANEL] * SCALE
        upper_one, inverse_one = factor(gram)
        factor_first_ref[...] = upper_one
        basis[:PANEL] = nn(inverse_one, powers[:PANEL, :])
        mix_ref[...] = inverse_one[PANEL - RHS :]

    def mix_early():
        for k in range(1, STEPS):
            basis[PANEL + (k - 1) * RHS : PANEL + k * RHS] = nn(mix_ref[...], powers[k * RHS : k * RHS + PANEL])
        both_ref[: PANEL + early, :early] = nt(basis[: PANEL + early], basis[PANEL : PANEL + early])

    def lay_out(value, turn, out_ref):
        n = value.shape[0]
        low = lax.broadcasted_iota(jnp.int32, (OWN, 2 * BS), 1) < BS
        for b in range(OWN):
            pair = value[:, b // 2 * 2 * BS : (b // 2 + 1) * 2 * BS]
            turn[:, b, :] = pair if b % 2 == 0 else pltpu.roll(pair, BS, 1)
        for p in range(0, n, 2):
            out_ref[:, p * BS : (p + 2) * BS] = jnp.where(low, turn[p], pltpu.roll(turn[p + 1], BS, 1))

    early = NEW - RHS
    tiles_one = PANEL // 8
    for t in range(STEPS):
        for h in range(HALVES):
            apply(t, h)
    gram_first()
    apply(4, 0)
    apply(4, 1)
    sum_second(0, tiles_one)
    apply(5, 0)
    apply(5, 1)
    sum_third(0, tiles_one)
    apply(6, 0)
    apply(6, 1)
    factor_one()
    apply(7, 0, [mix_early])
    apply(7, 1, [lambda: lay_out(basis[:PANEL], turn_first, first_ref)])
    last = nn(mix_ref[...], powers[STEPS * RHS :])
    basis[PANEL + early :] = last
    both_ref[:, early:] = nt(basis[...], last)
    both_ref[PANEL + early :, :early] = nt(last, basis[PANEL : PANEL + early])

    both = both_ref[...]
    half = (PANEL + NEW) // 2
    tiles_two = half // 8
    wide = jnp.concatenate([both[:half], both[half:]], 1)
    for i in range(tiles_two):
        sum_in[1][i] = wide[i * 8 : (i + 1) * 8]
    sum_first(1, tiles_two)
    sum_second(1, tiles_two)
    sum_third(1, tiles_two)
    sum_end(1, tiles_two)
    wide = jnp.concatenate([sum_out[1][i] for i in range(tiles_two)], 0) * SCALE
    coupling = jnp.concatenate([wide[:, :NEW], wide[: PANEL - half, NEW:]], 0)
    square = wide[PANEL - half :, NEW:]
    coupling_ref[...] = coupling.T
    gram = square - tn(coupling, coupling)
    projected = basis[PANEL:] - tn(coupling, basis[:PANEL])
    upper_two, inverse_two = factor(gram)
    factor_second_ref[...] = upper_two
    lay_out(nn(inverse_two, projected), turn_second, second_ref)

    sum_sent(0, tiles_one)
    sum_sent(1, tiles_two)


def hand_over(*refs):
    n = len(refs) // 2
    copies = [pltpu.make_async_copy(refs[i], refs[n + i], refs[-1].at[i]) for i in range(n)]
    for copy in copies:
        copy.start()
    for copy in copies:
        copy.wait()


def per_device(start, stiff, convect, column_index, upwind):
    vmem = pl.BlockSpec(memory_space=pltpu.VMEM)
    hbm = pl.BlockSpec(memory_space=pl.ANY)
    f32 = jnp.float32
    rows = pltpu.VMEM((HALVES, OWN, 4, 128), f32)
    sums = lambda: [pltpu.VMEM((16, 8, 128), f32) for _ in range(2)]
    results = pl.pallas_call(
        kernel,
        out_shape=(
            jax.ShapeDtypeStruct((OWN, PANEL * BS), f32),
            jax.ShapeDtypeStruct((OWN, NEW * BS), f32),
            jax.ShapeDtypeStruct((PANEL, PANEL), f32),
            jax.ShapeDtypeStruct((NEW, PANEL), f32),
            jax.ShapeDtypeStruct((NEW, NEW), f32),
        ),
        in_specs=[vmem, hbm, hbm, hbm, hbm],
        out_specs=(vmem,) * 5,
        scratch_shapes=[
            [[pltpu.VMEM((GROUP, 4, 128), f32) for _ in range(HALVES)] for _ in range(POWERS)],
            rows,
            [rows for _ in range(POWERS)],
            [rows for _ in range(POWERS)],
            [[pltpu.VMEM((2, OWN, 4, 128), f32) for _ in range(HALVES)] for _ in range(POWERS)],
            pltpu.VMEM((OWN, BS, SLOTS * BS), f32),
            pltpu.VMEM((OWN, BS, BS), f32),
            pltpu.VMEM((OWN, BS, 8 * BS), f32),
            pltpu.VMEM((OWN, BS, 2 * BS), f32),
            pltpu.VMEM((OWN, PART, BS), f32),
            pltpu.VMEM((ALL, WIDE), f32),
            pltpu.VMEM((PANEL + NEW, WIDE), f32),
            pltpu.VMEM((RHS, PANEL), f32),
            pltpu.VMEM((PANEL + NEW, NEW), f32),
            pltpu.VMEM((PANEL, OWN, 2 * BS), f32),
            pltpu.VMEM((NEW, OWN, 2 * BS), f32),
            pltpu.VMEM((2, OWN, SLOTS), jnp.int32),
            pltpu.SMEM((OWN, SLOTS), jnp.int32),
            pltpu.SMEM((OWN, SLOTS), jnp.int32),
            pltpu.SMEM((OWN, SLOTS), jnp.int32),
            pltpu.SMEM((OWN, SLOTS), jnp.int32),
            sums(),
            sums(),
            sums(),
            sums(),
            pltpu.SemaphoreType.DMA((POWERS, HALVES)),
            pltpu.SemaphoreType.DMA((POWERS, HALVES)),
            pltpu.SemaphoreType.DMA((POWERS, HALVES, 2)),
            pltpu.SemaphoreType.DMA((POWERS, HALVES, 2)),
            pltpu.SemaphoreType.DMA((2,)),
            pltpu.SemaphoreType.DMA((2,)),
            pltpu.SemaphoreType.DMA((6,)),
            pltpu.SemaphoreType.DMA((2, 3)),
            pltpu.SemaphoreType.DMA((2, 3)),
        ],
        compiler_params=pltpu.CompilerParams(
            collective_id=0, has_side_effects=True, vmem_limit_bytes=56 << 20
        ),
    )(start, stiff, convect, column_index, upwind)
    first, second, factor_first, coupling, factor_second = pl.pallas_call(
        hand_over,
        out_shape=tuple(jax.ShapeDtypeStruct(x.shape, f32) for x in results),
        in_specs=[vmem] * len(results),
        out_specs=(hbm,) * len(results),
        scratch_shapes=[pltpu.SemaphoreType.DMA((len(results),))],
    )(*results)
    return first, second, factor_first, coupling.T, factor_second


def solution(mesh):
    return jax.shard_map(
        per_device,
        mesh=mesh,
        in_specs=(
            P(("row", "col"), None),
            P(("row", "col"), None, None),
            P(("row", "col"), None, None),
            P(("row", "col"), None),
            P(("row", "col"), None),
        ),
        out_specs=(P(("row", "col"), None), P(("row", "col"), None), P(), P(), P()),
        check_vma=False,
    )
```

time: 115 us -> 107 us (0.930)
  local copies, waits for them, and re-layouts: 7.19 us -> 0 us
    reshape x7 -> x0, local copies, waits for them, and re-layouts: 4.32 us -> none  [the longest x4 2.71 us: per_device(): basis.reshape(-1, OWN, BS).transpose(1, 0, 2).reshape(OWN, -1)]
    unnamed x9 -> x0, local copies, waits for them, and re-layouts: 2.76 us -> none
    pallas_call x1 -> x2, Pallas kernels: 107 us -> 106 us  [the longest x1 104 us: per_device(): pl.pallas_call(kernel, out_shape=(jax.ShapeDtypeStruct((OWN, PANEL * BS),...]
where the time goes in v3:
time: 107 us
  Pallas kernels  106 us (99%)
    pallas_call x1, Pallas kernels, per_device(): pl.pallas_call(kernel, out_shape=(jax.ShapeDtypeStruct((OWN, PANEL * BS),...  104 us

profile of v3, /device:TPU:1, one launch (start us, length us, event | category | flops | bytes accessed | tf_op | source)
XLA Modules:
  0.0 106.8 jit_solution(9148375337727419377)
XLA Ops:
  0.6 104.2 %shard_map.92 = (f32[8,5120]{1,0:T(8,128)}, f32[8,4096]{1,0:T(8,128)}, f32[80,80]{1,0:T(8,128)}, f32[64,80]{1,0:T(8,128)}, f32[64,64]{1,0:T(8,128)}) custom-call(f32[8,1024]{1,0:T(8,128)} %start_ref.1, f32[8,64,576]{2,1,0:T(8,128)} %stiff_hbm.1, f32[8,64,64]{2,1,0:T(8,128)} %convect_hbm.1, s32[8,9]{1,0:T(8,128)} %index_hbm.1, s32[8,9]{1,0:T(8,128)} %upwind_hbm.1), custom_call_target="tpu_custom_call" | custom-call | tf_op jit(solution)/shard_map/pallas_call | solution.py:368
  104.8 1.8 %shard_map.93 = (f32[8,5120]{1,0:T(8,128)}, f32[8,4096]{1,0:T(8,128)}, f32[80,80]{1,0:T(8,128)}, f32[64,80]{1,0:T(8,128)}, f32[64,64]{1,0:T(8,128)}) custom-call(f32[8,5120]{1,0:T(8,128)} %get-tuple-element.15.refs_0_, f32[8,4096]{1,0:T(8,128)} %get-tuple-element.16.refs_1_, f32[80,80]{1,0:T(8,128)} %get-tuple-element.17.refs_2_, ...), custom_call_target="tpu_custom_call" | custom-call | tf_op jit(solution)/shard_map/pallas_call | solution.py:419

commit v4 on v3

--- a/solution.py
+++ b/solution.py
@@ -44,6 +44,24 @@
 
 def tn(a, b):
     return dot(a, b, ((0,), (0,)))
+
+
+def parts(x):
+    high = x.astype(jnp.bfloat16).astype(jnp.float32)
+    rest = x - high
+    middle = rest.astype(jnp.bfloat16).astype(jnp.float32)
+    return [high, middle, rest - middle]
+
+
+def weight_parts(x):
+    return jnp.concatenate(parts(x), 0).astype(jnp.bfloat16)
+
+
+def product(near, weights):
+    left = jnp.concatenate(parts(near) + [jnp.zeros_like(near)], 0).astype(jnp.bfloat16)
+    every = lax.dot_general(left, weights, (((1,), (1,)), ((), ())), preferred_element_type=jnp.float32)
+    total = every[16:24] + every[8:16] + every[:8]
+    return total[:, 2 * BS :] + total[:, BS : 2 * BS] + total[:, :BS]
 
 
 def local_row(index):
@@ -225,11 +243,10 @@
         flags[0] = flags[0] - total
         convect = convect_ref[b]
         blocks = [stiff_ref[b, :, j * BS : (j + 1) * BS] + flags[j] * convect for j in range(SLOTS)]
-        for j in range(0, 6, 2):
-            w_main[b, :, j * BS : (j + 2) * BS] = jnp.concatenate(blocks[j : j + 2], 1)
-        w_main[b, :, 6 * BS : 8 * BS] = jnp.concatenate([blocks[6], jnp.zeros_like(convect)], 1)
-        near_far = [jnp.where(odd == 0, blocks[8], blocks[7]), jnp.where(odd == 0, blocks[7], blocks[8])]
-        w_far[b] = jnp.concatenate(near_far, 1)
+        blocks.insert(7, jnp.zeros_like(convect))
+        w_main[b] = weight_parts(jnp.concatenate(blocks[:8], 1))
+        near_far = [jnp.where(odd == 0, blocks[9], blocks[8]), jnp.where(odd == 0, blocks[8], blocks[9])]
+        w_far[b] = weight_parts(jnp.concatenate(near_far, 1))
 
     arrived(index_in.at[0], index_recv.at[0])
     arrived(index_in.at[1], index_recv.at[1])
@@ -255,14 +272,15 @@
             tiles = [f[col * OWN + b]] + [f[local_row(index_ref[b, j])] for j in range(1, 7)]
             tiles.append(jnp.zeros_like(tiles[0]))
             near = jnp.concatenate([side_by_side(tiles[j], tiles[j + 1]) for j in range(0, 8, 2)], 1)
-            partial[b] = nt(near, w_main[b])
+            partial[b] = product(near, w_main[b])
         arrived(rows_twin[t].at[h], far_recv.at[t, h, 1])
         for call in beside:
             call()
         arrived(rows_far[t].at[h], far_recv.at[t, h, 0])
         results = []
         for b in range(OWN):
-            result = partial[b] + nt(side_by_side(rows_twin[t][h, b], rows_far[t][h, b]), w_far[b])
+            near = side_by_side(rows_twin[t][h, b], rows_far[t][h, b])
+            result = partial[b] + product(near, w_far[b])
             results.append(result)
             if t + 1 < POWERS:
                 field[t + 1][h][col * OWN + b] = jnp.concatenate([result[:4], result[4:]], 1)
@@ -384,8 +402,8 @@
             [[pltpu.VMEM((2, OWN, 4, 128), f32) for _ in range(HALVES)] for _ in range(POWERS)],
             pltpu.VMEM((OWN, BS, SLOTS * BS), f32),
             pltpu.VMEM((OWN, BS, BS), f32),
-            pltpu.VMEM((OWN, BS, 8 * BS), f32),
-            pltpu.VMEM((OWN, BS, 2 * BS), f32),
+            pltpu.VMEM((OWN, 3 * BS, 8 * BS), jnp.bfloat16),
+            pltpu.VMEM((OWN, 3 * BS, 2 * BS), jnp.bfloat16),
             pltpu.VMEM((OWN, PART, BS), f32),
             pltpu.VMEM((ALL, WIDE), f32),
             pltpu.VMEM((PANEL + NEW, WIDE), f32),

time: 107 us -> 105 us (0.981)
  Pallas kernels: 106 us -> 104 us
    pallas_call x1, Pallas kernels: 104 us -> 103 us  [per_device(): pl.pallas_call(kernel, out_shape=(jax.ShapeDtypeStruct((OWN, PANEL * BS),...]
where the time goes in v4:
time: 105 us
  Pallas kernels  104 us (99%)
    pallas_call x1, Pallas kernels, per_device(): pl.pallas_call(kernel, out_shape=(jax.ShapeDtypeStruct((OWN, PANEL * BS),...  103 us

profile of v4, /device:TPU:1, one launch (start us, length us, event | category | flops | bytes accessed | tf_op | source)
XLA Modules:
  0.0 105.2 jit_solution(6059699451467114848)
XLA Ops:
  0.6 102.6 %shard_map.92 = (f32[8,5120]{1,0:T(8,128)}, f32[8,4096]{1,0:T(8,128)}, f32[80,80]{1,0:T(8,128)}, f32[64,80]{1,0:T(8,128)}, f32[64,64]{1,0:T(8,128)}) custom-call(f32[8,1024]{1,0:T(8,128)} %start_ref.1, f32[8,64,576]{2,1,0:T(8,128)} %stiff_hbm.1, f32[8,64,64]{2,1,0:T(8,128)} %convect_hbm.1, s32[8,9]{1,0:T(8,128)} %index_hbm.1, s32[8,9]{1,0:T(8,128)} %upwind_hbm.1), custom_call_target="tpu_custom_call" | custom-call | tf_op jit(solution)/shard_map/pallas_call | solution.py:386
  103.2 1.8 %shard_map.93 = (f32[8,5120]{1,0:T(8,128)}, f32[8,4096]{1,0:T(8,128)}, f32[80,80]{1,0:T(8,128)}, f32[64,80]{1,0:T(8,128)}, f32[64,64]{1,0:T(8,128)}) custom-call(f32[8,5120]{1,0:T(8,128)} %get-tuple-element.15.refs_0_, f32[8,4096]{1,0:T(8,128)} %get-tuple-element.16.refs_1_, f32[80,80]{1,0:T(8,128)} %get-tuple-element.17.refs_2_, ...), custom_call_target="tpu_custom_call" | custom-call | tf_op jit(solution)/shard_map/pallas_call | solution.py:437

commit v5 on v4

--- a/solution.py
+++ b/solution.py
@@ -282,6 +282,7 @@
             near = side_by_side(rows_twin[t][h, b], rows_far[t][h, b])
             result = partial[b] + product(near, w_far[b])
             results.append(result)
+        for b, result in enumerate(results):
             if t + 1 < POWERS:
                 field[t + 1][h][col * OWN + b] = jnp.concatenate([result[:4], result[4:]], 1)
         if t + 1 < POWERS:

time: 105 us -> 105 us (level)
  no operation moved by 1% of the time
where the time goes in v5:
time: 105 us
  Pallas kernels  104 us (99%)
    pallas_call x1, Pallas kernels, per_device(): pl.pallas_call(kernel, out_shape=(jax.ShapeDtypeStruct((OWN, PANEL * BS),...  103 us

profile of v5, /device:TPU:1, one launch (start us, length us, event | category | flops | bytes accessed | tf_op | source)
XLA Modules:
  0.0 105.2 jit_solution(6059699451467114848)
XLA Ops:
  0.6 102.6 %shard_map.92 = (f32[8,5120]{1,0:T(8,128)}, f32[8,4096]{1,0:T(8,128)}, f32[80,80]{1,0:T(8,128)}, f32[64,80]{1,0:T(8,128)}, f32[64,64]{1,0:T(8,128)}) custom-call(f32[8,1024]{1,0:T(8,128)} %start_ref.1, f32[8,64,576]{2,1,0:T(8,128)} %stiff_hbm.1, f32[8,64,64]{2,1,0:T(8,128)} %convect_hbm.1, s32[8,9]{1,0:T(8,128)} %index_hbm.1, s32[8,9]{1,0:T(8,128)} %upwind_hbm.1), custom_call_target="tpu_custom_call" | custom-call | tf_op jit(solution)/shard_map/pallas_call | solution.py:387
  103.2 1.8 %shard_map.93 = (f32[8,5120]{1,0:T(8,128)}, f32[8,4096]{1,0:T(8,128)}, f32[80,80]{1,0:T(8,128)}, f32[64,80]{1,0:T(8,128)}, f32[64,64]{1,0:T(8,128)}) custom-call(f32[8,5120]{1,0:T(8,128)} %get-tuple-element.15.refs_0_, f32[8,4096]{1,0:T(8,128)} %get-tuple-element.16.refs_1_, f32[80,80]{1,0:T(8,128)} %get-tuple-element.17.refs_2_, ...), custom_call_target="tpu_custom_call" | custom-call | tf_op jit(solution)/shard_map/pallas_call | solution.py:438

commit v6 on v5

--- a/solution.py
+++ b/solution.py
@@ -114,7 +114,7 @@
 def kernel(
     start_ref, stiff_hbm, convect_hbm, index_hbm, upwind_hbm,
     first_ref, second_ref, factor_first_ref, coupling_ref, factor_second_ref,
-    field, start_tiles, rows_twin, rows_far, give, stiff_ref, convect_ref, w_main, w_far, partial, powers, basis, mix_ref, both_ref, turn_first, turn_second,
+    field, start_tiles, rows_twin, rows_far, give, stiff_ref, convect_ref, w_main, w_far, partial, powers, basis, mix_ref, both_ref, turn_first, turn_second, first_out,
     index_in, index_ref, upwind_ref, index_twin, index_far,
     sum_in, sum_a, sum_b, sum_out,
     send_sem, recv_sem, far_send, far_recv, index_send, index_recv, local_sem,
@@ -339,7 +339,14 @@
     apply(6, 1)
     factor_one()
     apply(7, 0, [mix_early])
-    apply(7, 1, [lambda: lay_out(basis[:PANEL], turn_first, first_ref)])
+    leave = pltpu.make_async_copy(first_out, first_ref, local_sem.at[6])
+
+    def first_leaves():
+        lay_out(basis[:PANEL], turn_first, first_out)
+        leave.start()
+
+    apply(7, 1, [first_leaves])
+    leave.wait()
     last = nn(mix_ref[...], powers[STEPS * RHS :])
     basis[PANEL + early :] = last
     both_ref[:, early:] = nt(basis[...], last)
@@ -394,7 +401,7 @@
             jax.ShapeDtypeStruct((NEW, NEW), f32),
         ),
         in_specs=[vmem, hbm, hbm, hbm, hbm],
-        out_specs=(vmem,) * 5,
+        out_specs=(hbm,) + (vmem,) * 4,
         scratch_shapes=[
             [[pltpu.VMEM((GROUP, 4, 128), f32) for _ in range(HALVES)] for _ in range(POWERS)],
             rows,
@@ -412,6 +419,7 @@
             pltpu.VMEM((PANEL + NEW, NEW), f32),
             pltpu.VMEM((PANEL, OWN, 2 * BS), f32),
             pltpu.VMEM((NEW, OWN, 2 * BS), f32),
+            pltpu.VMEM((OWN, PANEL * BS), f32),
             pltpu.VMEM((2, OWN, SLOTS), jnp.int32),
             pltpu.SMEM((OWN, SLOTS), jnp.int32),
             pltpu.SMEM((OWN, SLOTS), jnp.int32),
@@ -427,7 +435,7 @@
             pltpu.SemaphoreType.DMA((POWERS, HALVES, 2)),
             pltpu.SemaphoreType.DMA((2,)),
             pltpu.SemaphoreType.DMA((2,)),
-            pltpu.SemaphoreType.DMA((6,)),
+            pltpu.SemaphoreType.DMA((7,)),
             pltpu.SemaphoreType.DMA((2, 3)),
             pltpu.SemaphoreType.DMA((2, 3)),
         ],

time: 105 us -> 105 us (level)
  no operation moved by 1% of the time
where the time goes in v6:
time: 105 us
  Pallas kernels  104 us (99%)
    pallas_call x1, Pallas kernels, per_device(): pl.pallas_call(kernel, out_shape=(jax.ShapeDtypeStruct((OWN, PANEL * BS),...  102 us

profile of v6, /device:TPU:1, one launch (start us, length us, event | category | flops | bytes accessed | tf_op | source)
XLA Modules:
  0.0 104.6 jit_solution(37202685623112537)
XLA Ops:
  0.6 102.0 %shard_map.92 = (f32[8,5120]{1,0:T(8,128)}, f32[8,4096]{1,0:T(8,128)}, f32[80,80]{1,0:T(8,128)}, f32[64,80]{1,0:T(8,128)}, f32[64,64]{1,0:T(8,128)}) custom-call(f32[8,1024]{1,0:T(8,128)} %start_ref.1, f32[8,64,576]{2,1,0:T(8,128)} %stiff_hbm.1, f32[8,64,64]{2,1,0:T(8,128)} %convect_hbm.1, s32[8,9]{1,0:T(8,128)} %index_hbm.1, s32[8,9]{1,0:T(8,128)} %upwind_hbm.1), custom_call_target="tpu_custom_call" | custom-call | tf_op jit(solution)/shard_map/pallas_call | solution.py:394
  102.7 1.8 %shard_map.93 = (f32[8,5120]{1,0:T(8,128)}, f32[8,4096]{1,0:T(8,128)}, f32[80,80]{1,0:T(8,128)}, f32[64,80]{1,0:T(8,128)}, f32[64,64]{1,0:T(8,128)}) custom-call(f32[8,5120]{1,0:T(8,128)} %get-tuple-element.15.refs_0_, f32[8,4096]{1,0:T(8,128)} %get-tuple-element.16.refs_1_, f32[80,80]{1,0:T(8,128)} %get-tuple-element.17.refs_2_, ...), custom_call_target="tpu_custom_call" | custom-call | tf_op jit(solution)/shard_map/pallas_call | solution.py:446
